TPU v7x, 32 devices: a whole 2x2x4 slice. The times are simulated.
32 devices in a mesh: expert: 8 (over y, x, core), fsdp: 4 (over z).
Axes of the slice: x: 2, y: 2, z: 4, core: 2. Of those that a mesh axis runs over, the one named last changes fastest.
Arguments:
- tokens: bfloat16 [8192, 2048], P(('expert', 'fsdp')), may hold values from -6 to 6
- cotangent: bfloat16 [8192, 2048], P(('expert', 'fsdp')), may hold values from -6 to 6
- lengths: int32 [64], replicated, may hold values from 1 to 224, as said below
- owners: int32 [64], replicated, may hold values from 0 to 31, as said below
- routes: int32 [8192, 8], P(('expert', 'fsdp')), may hold values from 0 to 31, all different within a row; in each aligned block of 256 rows (0 to 255, 256 to 511, ...) at most 80 rows name the same one
- w_query: bfloat16 [2048, 4096], P(('expert', 'fsdp')), may hold values from -0.125 to 0.125
- key_weight: bfloat16 [2048, 512], P(('expert', 'fsdp')), may hold values from -0.125 to 0.125
- value_weight: bfloat16 [2048, 512], P(('expert', 'fsdp')), may hold values from -0.125 to 0.125
- w_out: bfloat16 [4096, 2048], P(('expert', 'fsdp')), may hold values from -0.375 to 0.375
- w_router: bfloat16 [2048, 32], P(('expert', 'fsdp')), may hold values from -0.0625 to 0.0625
- norm_gains: bfloat16 [4352], P(('expert', 'fsdp')), may hold values from 0.099609375 to 1.8984375
- w_gate: bfloat16 [32, 2048, 768], P(('expert', 'fsdp')), may hold values from -0.125 to 0.125
- w_up: bfloat16 [32, 2048, 768], P(('expert', 'fsdp')), may hold values from -0.125 to 0.125
- w_down: bfloat16 [32, 768, 2048], P(('expert', 'fsdp')), may hold values from -0.875 to 0.875
Outputs:
- block_out: bfloat16 [8192, 2048], P(('expert', 'fsdp'))
- grad_tokens: float32 [8192, 2048], P(('expert', 'fsdp'))
- grad_query: float32 [2048, 4096], P(('expert', 'fsdp'))
- grad_key: float32 [2048, 512], P(('expert', 'fsdp'))
- grad_value: float32 [2048, 512], P(('expert', 'fsdp'))
- grad_out: float32 [4096, 2048], P(('expert', 'fsdp'))
- grad_router: float32 [2048, 32], P(('expert', 'fsdp'))
- grad_gains: float32 [4352], P(('expert', 'fsdp'))
- grad_gate: float32 [32, 2048, 768], P(('expert', 'fsdp'))
- grad_up: float32 [32, 2048, 768], P(('expert', 'fsdp'))
- grad_down: float32 [32, 768, 2048], P(('expert', 'fsdp'))
Inputs may be any that keep to these rules, and one draw needn't show every extreme that they name: `lengths`: sequences 2 i and 2 i + 1 have the same owner, every device owns exactly two sequences, and the two sequences of a device have at most 256 tokens together; the longest sequence has 224 tokens. `owners`: every device owns exactly two sequences. `routes`: the 8 experts of a slot differ; within the slots of one device (aligned blocks of 256 rows) no expert is named by more than 80 rows, padding slots included.
All inputs are finite; a program needn't handle non-finite values.
Results may differ from a plain program's by a relative error of at most 0.018.
Values may be sent and summed in bfloat16 or wider, within the bound.
A program may use at most 384 MiB of HBM per device.

v0:
```python
from functools import partial

import jax
import jax.numpy as jnp
from jax import lax
from jax.sharding import PartitionSpec as P

EPSILON = 1e-06


def rms_norm(values, gain_row):
    return (
        values * lax.rsqrt(jnp.mean(values * values, axis=-1, keepdims=True) + EPSILON) * gain_row
    )


def rotate(values, token_position):
    half_size = values.shape[-1] // 2
    frequency = jnp.power(
        1000000.0, -2.0 * jnp.arange(half_size, dtype=jnp.float32) / values.shape[-1]
    )
    angles = token_position.astype(jnp.float32)[:, None] * frequency[None, :]
    cosine = jnp.cos(angles)[:, None, :]
    sine_val = jnp.sin(angles)[:, None, :]
    first_half = values[..., :half_size]
    second_half = values[..., half_size:]
    return jnp.concatenate(
        [
            first_half * cosine - second_half * sine_val,
            second_half * cosine + first_half * sine_val,
        ],
        axis=-1,
    )


def prepare_attention(token_position, head_count, raw_rows, gain_row):
    shaped = raw_rows.reshape(raw_rows.shape[0], head_count, -1)
    return rotate(rms_norm(shaped, gain_row), token_position)


def layout(lengths, owners, device, row_count):
    seq_order = jnp.arange(lengths.shape[0], dtype=jnp.int32)
    owned = (owners == device).astype(jnp.int32)
    earlier = (seq_order[None, :] < seq_order[:, None]).astype(jnp.int32)
    starts = jnp.sum(earlier * (owned * lengths)[None, :], axis=1)
    row_index = jnp.arange(row_count, dtype=jnp.int32)
    inside = (
        owned[None, :]
        * (row_index[:, None] >= starts[None, :]).astype(jnp.int32)
        * (row_index[:, None] < (starts + lengths)[None, :]).astype(jnp.int32)
    )
    live_rows = jnp.sum(inside, axis=1)
    segment = jnp.sum(inside * (seq_order[None, :] + 1), axis=1) - 1
    token_position = jnp.sum(inside * (row_index[:, None] - starts[None, :]), axis=1)
    return (live_rows, segment, token_position)


def allowed_mask(segment):
    row_index = jnp.arange(segment.shape[0], dtype=jnp.int32)
    same_seq = (
        (segment[:, None] == segment[None, :])
        & (segment[:, None] >= 0)
        & (row_index[None, :] <= row_index[:, None])
    )
    return same_seq | (row_index[:, None] == row_index[None, :])


def slot_table(routes, live_rows, experts):
    flat_routes = routes.reshape(-1)
    route_live = jnp.repeat(live_rows, routes.shape[1])
    onehot = (flat_routes[:, None] == jnp.arange(experts, dtype=jnp.int32)[None, :]).astype(
        jnp.int32
    ) * route_live[:, None]
    before = jnp.cumsum(onehot, axis=0) - onehot
    slot_of = jnp.sum(before * onehot, axis=1)
    return (slot_of.reshape(routes.shape), route_live.reshape(routes.shape))


def gate_values(routes, logits):
    probs_all = jax.nn.softmax(logits, axis=-1)
    picked = jnp.take_along_axis(probs_all, routes, axis=1)
    return picked / jnp.sum(picked, axis=1, keepdims=True)


def dot_last(left_side, right_side):
    return lax.dot_general(
        left_side, right_side, (((1,), (1,)), ((), ())), preferred_element_type=jnp.float32
    )


def dot_first(left_side, right_side):
    return lax.dot_general(
        left_side, right_side, (((0,), (0,)), ((), ())), preferred_element_type=jnp.float32
    )


def attention_scores(query_b, key_b, allowed, score_scale):
    scores = (
        jnp.einsum("tkgd,skd->kgts", query_b, key_b, preferred_element_type=jnp.float32)
        * score_scale
    )
    return jnp.where(allowed[None, None], scores, -1e30)


def send_rows(buffer):
    return lax.all_to_all(buffer, ("expert", "fsdp"), split_axis=0, concat_axis=0, tiled=True)


def return_rows(buffer):
    return lax.all_to_all(buffer, ("expert", "fsdp"), split_axis=0, concat_axis=0, tiled=True)


def send_grads(buffer):
    return lax.all_to_all(buffer, ("expert", "fsdp"), split_axis=0, concat_axis=0, tiled=True)


def return_grads(buffer):
    return lax.all_to_all(buffer, ("expert", "fsdp"), split_axis=0, concat_axis=0, tiled=True)


def local(
    tokens,
    cotangent,
    lengths,
    owners,
    routes,
    w_query,
    key_weight,
    value_weight,
    w_out,
    w_router,
    norm_gains,
    w_gate,
    w_up,
    w_down,
):
    gathered = (
        lax.all_gather(w_query, ("expert", "fsdp"), axis=0, tiled=True),
        lax.all_gather(key_weight, ("expert", "fsdp"), axis=0, tiled=True),
        lax.all_gather(value_weight, ("expert", "fsdp"), axis=0, tiled=True),
        lax.all_gather(w_out, ("expert", "fsdp"), axis=0, tiled=True),
        lax.all_gather(w_router, ("expert", "fsdp"), axis=0, tiled=True),
        lax.all_gather(norm_gains, ("expert", "fsdp"), axis=0, tiled=True),
    )
    query_w, key_w, value_w, out_w, router_w, gain_vector = gathered
    row_count = tokens.shape[0]
    model_width = tokens.shape[1]
    head_size = gain_vector.shape[0] // 2 - model_width
    head_count = query_w.shape[1] // head_size
    kv_heads = key_w.shape[1] // head_size
    group_size = head_count // kv_heads
    experts = router_w.shape[1]
    top_count = routes.shape[1]
    capacity = row_count * top_count * 5 // (4 * experts)
    score_scale = head_size ** (-0.5)
    gain_float = gain_vector.astype(jnp.float32)
    gain_one = gain_float[:model_width]
    gain_two = gain_float[model_width : 2 * model_width]
    query_norm_gain = gain_float[2 * model_width : 2 * model_width + head_size]
    key_norm_gain = gain_float[2 * model_width + head_size :]
    device = lax.axis_index(("expert", "fsdp"))
    live_rows, segment, token_position = layout(lengths, owners, device, row_count)
    live_col = live_rows.astype(jnp.float32)[:, None]
    allowed = allowed_mask(segment)
    inputs = tokens.astype(jnp.float32)
    normed_inputs, norm_back = jax.vjp(rms_norm, inputs, gain_one)
    normed_b = normed_inputs.astype(jnp.bfloat16)
    query_projected = jnp.dot(normed_b, query_w, preferred_element_type=jnp.float32)
    key_projected = jnp.dot(normed_b, key_w, preferred_element_type=jnp.float32)
    value_b = (
        jnp.dot(normed_b, value_w, preferred_element_type=jnp.float32)
        .astype(jnp.bfloat16)
        .reshape(row_count, kv_heads, head_size)
    )
    query_normalized, query_back = jax.vjp(
        partial(prepare_attention, token_position, head_count), query_projected, query_norm_gain
    )
    key_normalized, key_back = jax.vjp(
        partial(prepare_attention, token_position, kv_heads), key_projected, key_norm_gain
    )
    query_b = query_normalized.astype(jnp.bfloat16).reshape(
        row_count, kv_heads, group_size, head_size
    )
    key_b = key_normalized.astype(jnp.bfloat16)
    scores = attention_scores(query_b, key_b, allowed, score_scale)
    row_peak = jnp.max(scores, axis=-1, keepdims=True)
    row_total = jnp.sum(jnp.exp(scores - row_peak), axis=-1, keepdims=True)
    log_total = row_peak + jnp.log(row_total)
    attend_b = jnp.exp(scores - log_total).astype(jnp.bfloat16)
    mixed_b = (
        jnp.einsum("kgts,skd->tkgd", attend_b, value_b, preferred_element_type=jnp.float32)
        .astype(jnp.bfloat16)
        .reshape(row_count, head_count * head_size)
    )
    attn_rows = jnp.dot(mixed_b, out_w, preferred_element_type=jnp.float32)
    hidden = inputs + live_col * attn_rows
    normed_two, norm_two_back = jax.vjp(rms_norm, hidden, gain_two)
    normed_two_b = normed_two.astype(jnp.bfloat16)
    logits = jnp.dot(normed_two_b, router_w, preferred_element_type=jnp.float32)
    gate_weights, gate_back = jax.vjp(partial(gate_values, routes), logits)
    slot_of, route_live = slot_table(routes, live_rows, experts)
    live_f = route_live.astype(jnp.float32)
    rows_in = (
        jnp.broadcast_to(normed_two_b[:, None, :], (row_count, top_count, model_width))
        * route_live.astype(jnp.bfloat16)[:, :, None]
    )
    buffer = (
        jnp.zeros((experts, capacity, model_width), jnp.bfloat16).at[routes, slot_of].add(rows_in)
    )
    received = send_rows(buffer)
    expert_rows = received.reshape(-1, model_width)
    gate_part = jnp.dot(expert_rows, w_gate[0], preferred_element_type=jnp.float32)
    up_part = jnp.dot(expert_rows, w_up[0], preferred_element_type=jnp.float32)
    activated = jax.nn.silu(gate_part)
    inner_b = (activated * up_part).astype(jnp.bfloat16)
    result_b = (
        jnp.dot(inner_b, w_down[0], preferred_element_type=jnp.float32)
        .astype(jnp.bfloat16)
        .reshape(received.shape)
    )
    returned = return_rows(result_b)
    picked = returned[routes, slot_of].astype(jnp.float32)
    weighted = gate_weights * live_f
    block_out = (hidden + jnp.sum(weighted[:, :, None] * picked, axis=1)).astype(jnp.bfloat16)
    upstream = cotangent.astype(jnp.float32)
    grad_picked_b = (weighted[:, :, None] * upstream[:, None, :]).astype(jnp.bfloat16)
    grad_gates = live_f * jnp.sum(upstream[:, None, :] * picked, axis=-1)
    grad_buffer = (
        jnp.zeros((experts, capacity, model_width), jnp.bfloat16)
        .at[routes, slot_of]
        .add(grad_picked_b)
    )
    grad_result = send_grads(grad_buffer).reshape(-1, model_width)
    grad_inner = dot_last(grad_result, w_down[0])
    grad_wdown = dot_first(inner_b, grad_result)
    sigmoid_g = jax.nn.sigmoid(gate_part)
    grad_gate_b = (grad_inner * up_part * sigmoid_g * (1.0 + gate_part * (1.0 - sigmoid_g))).astype(
        jnp.bfloat16
    )
    grad_up_b = (grad_inner * activated).astype(jnp.bfloat16)
    grad_wgate = dot_first(expert_rows, grad_gate_b)
    grad_wup = dot_first(expert_rows, grad_up_b)
    grad_rows_b = (
        (dot_last(grad_gate_b, w_gate[0]) + dot_last(grad_up_b, w_up[0]))
        .astype(jnp.bfloat16)
        .reshape(received.shape)
    )
    grad_back = return_grads(grad_rows_b)
    grad_normed_two = jnp.sum(
        grad_back[routes, slot_of].astype(jnp.float32) * live_f[:, :, None], axis=1
    )
    (grad_logits,) = gate_back(grad_gates)
    grad_logits_b = grad_logits.astype(jnp.bfloat16)
    grad_router = dot_first(normed_two_b, grad_logits_b)
    grad_normed_two = grad_normed_two + dot_last(grad_logits_b, router_w)
    grad_hidden_norm, grad_gain_two = norm_two_back(grad_normed_two)
    grad_hidden = upstream + grad_hidden_norm
    grad_attn_b = (live_col * grad_hidden).astype(jnp.bfloat16)
    grad_outw = dot_first(mixed_b, grad_attn_b)
    grad_mixed_b = (
        dot_last(grad_attn_b, out_w)
        .astype(jnp.bfloat16)
        .reshape(row_count, kv_heads, group_size, head_size)
    )
    scores = attention_scores(query_b, key_b, allowed, score_scale)
    attend = jnp.exp(scores - log_total)
    attend_b = attend.astype(jnp.bfloat16)
    grad_attend = jnp.einsum(
        "tkgd,skd->kgts", grad_mixed_b, value_b, preferred_element_type=jnp.float32
    )
    row_delta = jnp.sum(attend * grad_attend, axis=-1, keepdims=True)
    grad_scores_b = (attend * (grad_attend - row_delta)).astype(jnp.bfloat16)
    grad_query_n = (
        jnp.einsum("kgts,skd->tkgd", grad_scores_b, key_b, preferred_element_type=jnp.float32)
        * score_scale
    )
    grad_key_n = (
        jnp.einsum("kgts,tkgd->skd", grad_scores_b, query_b, preferred_element_type=jnp.float32)
        * score_scale
    )
    grad_value_b = (
        jnp.einsum("kgts,tkgd->skd", attend_b, grad_mixed_b, preferred_element_type=jnp.float32)
        .astype(jnp.bfloat16)
        .reshape(row_count, kv_heads * head_size)
    )
    grad_query_raw, grad_gain_query = query_back(
        grad_query_n.reshape(row_count, head_count, head_size)
    )
    grad_key_raw, grad_gain_key = key_back(grad_key_n)
    grad_query_b = grad_query_raw.astype(jnp.bfloat16)
    grad_key_b = grad_key_raw.astype(jnp.bfloat16)
    grad_queryw = dot_first(normed_b, grad_query_b)
    grad_keyw = dot_first(normed_b, grad_key_b)
    grad_valuew = dot_first(normed_b, grad_value_b)
    grad_normed = (
        dot_last(grad_query_b, query_w)
        + dot_last(grad_key_b, key_w)
        + dot_last(grad_value_b, value_w)
    )
    grad_inputs_norm, grad_gain_one = norm_back(grad_normed)
    grad_tokens = grad_hidden + grad_inputs_norm
    grad_gain_all = jnp.concatenate([grad_gain_one, grad_gain_two, grad_gain_query, grad_gain_key])
    grad_terms = (grad_queryw, grad_keyw, grad_valuew, grad_outw, grad_router, grad_gain_all)
    grad_shares = (
        lax.psum_scatter(grad_terms[0], ("expert", "fsdp"), scatter_dimension=0, tiled=True),
        lax.psum_scatter(grad_terms[1], ("expert", "fsdp"), scatter_dimension=0, tiled=True),
        lax.psum_scatter(grad_terms[2], ("expert", "fsdp"), scatter_dimension=0, tiled=True),
        lax.psum_scatter(grad_terms[3], ("expert", "fsdp"), scatter_dimension=0, tiled=True),
        lax.psum_scatter(grad_terms[4], ("expert", "fsdp"), scatter_dimension=0, tiled=True),
        lax.psum_scatter(grad_terms[5], ("expert", "fsdp"), scatter_dimension=0, tiled=True),
    )
    return (
        block_out,
        grad_tokens,
        grad_shares[0],
        grad_shares[1],
        grad_shares[2],
        grad_shares[3],
        grad_shares[4],
        grad_shares[5],
        grad_wgate[None],
        grad_wup[None],
        grad_wdown[None],
    )


def solution(mesh):
    return jax.shard_map(
        local,
        mesh=mesh,
        in_specs=(
            P(("expert", "fsdp"), None),
            P(("expert", "fsdp"), None),
            P(),
            P(),
            P(("expert", "fsdp"), None),
            P(("expert", "fsdp"), None),
            P(("expert", "fsdp"), None),
            P(("expert", "fsdp"), None),
            P(("expert", "fsdp"), None),
            P(("expert", "fsdp"), None),
            P(("expert", "fsdp")),
            P(("expert", "fsdp"), None, None),
            P(("expert", "fsdp"), None, None),
            P(("expert", "fsdp"), None, None),
        ),
        out_specs=(
            P(("expert", "fsdp"), None),
            P(("expert", "fsdp"), None),
            P(("expert", "fsdp"), None),
            P(("expert", "fsdp"), None),
            P(("expert", "fsdp"), None),
            P(("expert", "fsdp"), None),
            P(("expert", "fsdp"), None),
            P(("expert", "fsdp")),
            P(("expert", "fsdp"), None, None),
            P(("expert", "fsdp"), None, None),
            P(("expert", "fsdp"), None, None),
        ),
        check_vma=False,
    )
```

profile of v0, /device:TPU:0, one launch (start us, length us, event | category | flops | bytes accessed | tf_op | source)
XLA Modules:
  0.0 3346.6 jit_solution(13267863542655267689)
XLA Ops:
  14.6 15.9 reduce-window.6
  35.5 42.6 %all-reduce.4 = bf16[4352]{0:T(1024)(128)(2,1)S(1)} all-reduce(bf16[4352]{0:T(1024)(128)(2,1)S(1)} %dynamic-update-slice), channel_id=1, replica_groups=mesh['expert'=8,'fsdp'=4] {'expert','fsdp'}, use_global_device_ids=true, to_apply=%add.4 | all-reduce | flops 4352 | bytes 17408
  86.7 42.3 %all-gather.8.cloned.1.call-done = bf16[2048,512]{1,0:T(8,128)(2,1)} async-done(((bf16[64,512]{1,0:T(8,128)(2,1)}), bf16[2048,512]{1,0:T(8,128)(2,1)}) %all-gather.8.cloned.1.call-update) | async-done | bytes 2097168 | tf_op jit(solution)/shard_map/all_gather | solution.py:139
  139.8 105.9 %all-gather.10.cloned.1.call-done = bf16[2048,4096]{1,0:T(8,128)(2,1)} async-done(((bf16[64,4096]{1,0:T(8,128)(2,1)}), bf16[2048,4096]{1,0:T(8,128)(2,1)}) %all-gather.10.cloned.1.call-update) | async-done | bytes 16777232 | tf_op jit(solution)/shard_map/all_gather | solution.py:138
  280.2 81.5 %all-gather.12.cloned.1.call-done = bf16[4096,2048]{1,0:T(8,128)(2,1)} async-done(((bf16[128,2048]{1,0:T(8,128)(2,1)}), bf16[4096,2048]{1,0:T(8,128)(2,1)}) %all-gather.12.cloned.1.call-update) | async-done | bytes 16777232 | tf_op jit(solution)/shard_map/all_gather | solution.py:141
  376.0 33.8 %scatter_custom_fusion = bf16[2560,2048]{1,0:T(8,128)(2,1)} fusion(s32[2048]{0:T(1024)} %reshape.448, bf16[]{:T(256)} %constant.90.clone.1, bf16[256]{0:T(256)(128)(2,1)S(1)} %copy-done.87, bf16[256,2048]{1,0:T(8,128)(2,1)} %multiply_convert_fusion.5), kind=kCustom, calls=%fused_computation.22 | custom fusion | flops 8388608 | bytes 11535360
  413.9 292.7 %all-gather = bf16[32,64,32]{1,2,0:T(8,128)(2,1)S(1)} all-gather(bf16[1,64,32]{1,2,0:T(8,128)(2,1)S(1)} %bitcast.234), channel_id=1, replica_groups=mesh['expert'=8,'fsdp'=4] {'expert','fsdp'}, dimensions={0}, use_global_device_ids=true | all-gather | bytes 135168 | tf_op jit(solution)/shard_map/all_gather | solution.py:142
  712.7 16.8 gather_fusion.2
  730.5 33.5 %scatter_custom_fusion.1 = bf16[2560,2048]{1,0:T(8,128)(2,1)} fusion(s32[2048]{0:T(1024)} %reshape.448, f32[256,2048]{1,0:T(8,128)} %convert_element_type.132, f32[256,8]{1,0:T(8,128)S(1)} %copy.269, bf16[]{:T(256)} %constant.90.clone.1), kind=kCustom, calls=%fused_computation.16 | custom fusion | flops 12582912 | bytes 12591616
  767.9 13.9 fusion.26
  794.8 199.2 %all-to-all-done.2 = bf16[32,80,2048]{2,1,0:T(8,128)(2,1)} async-done(((bf16[32,80,2048]{2,1,0:T(8,128)(2,1)}), bf16[32,80,2048]{2,1,0:T(8,128)(2,1)}, u32[]{:S(2)}, u32[]{:S(2)}) %all-to-all-start.2) | async-done | bytes 10485792 | tf_op jit(solution)/shard_map/all_to_all | solution.py:114
  994.0 19.7 multiply_convert_fusion.1
  1050.5 16.6 add_convert_fusion
  1067.1 196.1 %all-to-all-done.1 = bf16[32,80,2048]{2,1,0:T(8,128)(2,1)} async-done(((bf16[32,80,2048]{2,1,0:T(8,128)(2,1)}), bf16[32,80,2048]{2,1,0:T(8,128)(2,1)}, u32[]{:S(2)}, u32[]{:S(2)}) %all-to-all-start.1) | async-done | bytes 10485792 | tf_op jit(solution)/shard_map/all_to_all | solution.py:110
  1281.7 50.9 %gather_fusion = bf16[2048,2048]{1,0:T(8,128)(2,1)} fusion(bf16[32,80,2048]{2,1,0:T(8,128)(2,1)} %all-to-all-done.1, s32[2048]{0:T(1024)S(1)} %reshape.430), kind=kCustom, calls=%fused_computation | custom fusion | bytes 16793600 | tf_op jit(solution)/shard_map/gather | solution.py:222
  1356.9 159.9 %all-to-all-done.3 = bf16[32,80,2048]{2,1,0:T(8,128)(2,1)} async-done(((bf16[32,80,2048]{2,1,0:T(8,128)(2,1)}), bf16[32,80,2048]{2,1,0:T(8,128)(2,1)}, u32[]{:S(2)}, u32[]{:S(2)}) %all-to-all-start.3) | async-done | bytes 10485792 | tf_op jit(solution)/shard_map/all_to_all | solution.py:118
  1516.8 51.1 %gather_fusion.1 = bf16[2048,2048]{1,0:T(8,128)(2,1)} fusion(bf16[32,80,2048]{2,1,0:T(8,128)(2,1)} %all-to-all-done.3, s32[2048]{0:T(1024)S(1)} %reshape.430), kind=kCustom, calls=%fused_computation.1 | custom fusion | bytes 16793600 | tf_op jit(solution)/shard_map/gather | solution.py:250
  1628.0 15.1 fusion.78
  1678.3 13.6 fusion.40
  1691.9 14.3 convolution_bitcast_fusion
  1750.0 47.9 %all-reduce.5 = f32[4352]{0:T(1024)S(1)} all-reduce(f32[4352]{0:T(1024)S(1)} %pad_maximum_fusion.3), channel_id=7, replica_groups=mesh['expert'=8,'fsdp'=4] {'expert','fsdp'}, use_global_device_ids=true, to_apply=%region_38.39.clone | all-reduce | flops 4352 | bytes 34816
  1804.5 107.1 %reduce-scatter.10.cloned.1.call-done = f32[64,512]{1,0:T(8,128)} async-done(((f32[2048,512]{1,0:T(8,128)}), f32[64,512]{1,0:T(8,128)}) %reduce-scatter.10.cloned.1.call-update) | async-done | bytes 131088 | tf_op jit(solution)/shard_map/reduce_scatter | solution.py:306
  1911.6 713.7 %reduce-scatter.14.cloned.1.call-done = f32[128,2048]{1,0:T(8,128)} async-done(((f32[4096,2048]{1,0:T(8,128)}), f32[128,2048]{1,0:T(8,128)}) %reduce-scatter.14.cloned.1.call-update) | async-done | bytes 1048592 | tf_op jit(solution)/shard_map/reduce_scatter | solution.py:308
  2625.3 714.3 %reduce-scatter.8.cloned.1.call-done = f32[64,4096]{1,0:T(8,128)} async-done(((f32[2048,4096]{1,0:T(8,128)}), f32[64,4096]{1,0:T(8,128)}) %reduce-scatter.8.cloned.1.call-update) | async-done | bytes 1048592 | tf_op jit(solution)/shard_map/reduce_scatter | solution.py:305
  (364 shorter events, 332.5 us)
Async XLA Ops:
  7.2 986.9 %copy-start = (bf16[1,768,2048]{2,1,0:T(8,128)(2,1)S(1)}, bf16[1,768,2048]{2,1,0:T(8,128)(2,1)}, u32[]{:S(2)}) copy-start(bf16[1,768,2048]{2,1,0:T(8,128)(2,1)} %param.27) | copy-start | bytes 9437188
  7.3 74.2 %all-gather.6.cloned.1.call-start = ((), (), s32[]{:S(2)}) async-start(), calls=%async_computation.9 | async-start | bytes 2162688 | tf_op jit(solution)/shard_map/all_gather | solution.py:140
  8.0 121.0 %all-gather.8.cloned.1.call-start = ((), (), s32[]{:S(2)}) async-start(), calls=%async_computation.10 | async-start | bytes 2162688 | tf_op jit(solution)/shard_map/all_gather | solution.py:139
  8.8 237.0 %all-gather.10.cloned.1.call-start = ((), (), s32[]{:S(2)}) async-start(), calls=%async_computation.11 | async-start | bytes 17301504 | tf_op jit(solution)/shard_map/all_gather | solution.py:138
  9.5 352.2 %all-gather.12.cloned.1.call-start = ((), (), s32[]{:S(2)}) async-start(), calls=%async_computation.12 | async-start | bytes 17301504 | tf_op jit(solution)/shard_map/all_gather | solution.py:141
  79.7 166.1 %copy-start.59 = (f32[256]{0:T(256)}, f32[256]{0:T(256)S(1)}, u32[]{:S(2)}) copy-start(f32[256]{0:T(256)S(1)} %fusion.72) | copy-start | bytes 3076
  80.8 164.9 %copy-start.45 = (f32[2048]{0:T(1024)}, f32[2048]{0:T(1024)S(1)}, u32[]{:S(2)}) copy-start(f32[2048]{0:T(1024)S(1)} %get-tuple-element.44) | copy-start | bytes 24580
  80.8 292.7 %copy-start.55 = (f32[2048]{0:T(1024)}, f32[2048]{0:T(1024)S(1)}, u32[]{:S(2)}) copy-start(f32[2048]{0:T(1024)S(1)} %get-tuple-element.43) | copy-start | bytes 24580
  80.9 191.9 %copy-start.27 = (pred[256,256]{0,1:T(8,128)(4,1)}, pred[256,256]{0,1:T(8,128)(4,1)S(1)}, u32[]{:S(2)}) copy-start(pred[256,256]{0,1:T(8,128)(4,1)S(1)} %fusion.58) | copy-start | bytes 196612
  81.5 183.0 %copy-start.23 = (f32[256,64]{1,0:T(8,128)}, f32[256,64]{1,0:T(8,128)S(1)}, u32[]{:S(2)}) copy-start(f32[256,64]{1,0:T(8,128)S(1)} %get-tuple-element.50) | copy-start | bytes 196612
  81.5 183.0 %copy-start.25 = (f32[256,64]{1,0:T(8,128)}, f32[256,64]{1,0:T(8,128)S(1)}, u32[]{:S(2)}) copy-start(f32[256,64]{1,0:T(8,128)S(1)} %get-tuple-element.51) | copy-start | bytes 196612
  137.5 116.8 %copy-start.66 = (f32[256,4]{0,1:T(4,128)}, f32[256,4]{0,1:T(4,128)S(1)}, u32[]{:S(2)}) copy-start(f32[256,4]{0,1:T(4,128)S(1)} %copy.258) | copy-start | bytes 12292
  137.5 116.7 %copy-start.61 = (f32[256,4]{0,1:T(4,128)}, f32[256,4]{0,1:T(4,128)S(1)}, u32[]{:S(2)}) copy-start(f32[256,4]{0,1:T(4,128)S(1)} %fusion.71) | copy-start | bytes 12292
  276.1 85.6 %copy-start.63 = (f32[256]{0:T(256)S(1)}, f32[256]{0:T(256)}, u32[]{:S(2)}) copy-start(f32[256]{0:T(256)} %get-tuple-element.53) | copy-start | bytes 3076
  409.8 354.2 %all-to-all-start = ((bf16[32,80,2048]{2,1,0:T(8,128)(2,1)}), bf16[32,80,2048]{2,1,0:T(8,128)(2,1)}, u32[]{:S(2)}, u32[]{:S(2)}) async-start(bf16[32,80,2048]{2,1,0:T(8,128)(2,1)} %bitcast.210), calls=%async_computation | async-start | bytes 20971520 | tf_op jit(solution)/shard_map/all_to_all | solution.py:106
  763.9 230.1 %all-to-all-start.2 = ((bf16[32,80,2048]{2,1,0:T(8,128)(2,1)}), bf16[32,80,2048]{2,1,0:T(8,128)(2,1)}, u32[]{:S(2)}, u32[]{:S(2)}) async-start(bf16[32,80,2048]{2,1,0:T(8,128)(2,1)} %bitcast.211), calls=%async_computation.2 | async-start | bytes 20971520 | tf_op jit(solution)/shard_map/all_to_all | solution.py:114
  1027.1 236.1 %all-to-all-start.1 = ((bf16[32,80,2048]{2,1,0:T(8,128)(2,1)}), bf16[32,80,2048]{2,1,0:T(8,128)(2,1)}, u32[]{:S(2)}, u32[]{:S(2)}) async-start(bf16[32,80,2048]{2,1,0:T(8,128)(2,1)} %bitcast.222), calls=%async_computation.1 | async-start | bytes 20971520 | tf_op jit(solution)/shard_map/all_to_all | solution.py:110
  1263.2 253.6 %all-to-all-start.3 = ((bf16[32,80,2048]{2,1,0:T(8,128)(2,1)}), bf16[32,80,2048]{2,1,0:T(8,128)(2,1)}, u32[]{:S(2)}, u32[]{:S(2)}) async-start(bf16[32,80,2048]{2,1,0:T(8,128)(2,1)} %bitcast.221), calls=%async_computation.3 | async-start | bytes 20971520 | tf_op jit(solution)/shard_map/all_to_all | solution.py:118
  1273.1 529.9 %reduce-scatter.16.cloned.1.call-start = ((), (), s32[]{:S(2)}) async-start(), calls=%async_computation.17 | async-start | bytes 1081344
  1356.9 447.6 %reduce-scatter.12.cloned.1.call-start = ((), (), s32[]{:S(2)}) async-start(), calls=%async_computation.15 | async-start | bytes 4325376 | tf_op jit(solution)/shard_map/reduce_scatter | solution.py:307
  1607.2 304.4 %reduce-scatter.10.cloned.1.call-start = ((), (), s32[]{:S(2)}) async-start(), calls=%async_computation.14 | async-start | bytes 4325376 | tf_op jit(solution)/shard_map/reduce_scatter | solution.py:306
  1626.5 998.9 %reduce-scatter.14.cloned.1.call-start = ((), (), s32[]{:S(2)}) async-start(), calls=%async_computation.16 | async-start | bytes 34603008 | tf_op jit(solution)/shard_map/reduce_scatter | solution.py:308
  1643.1 1696.5 %reduce-scatter.8.cloned.1.call-start = ((), (), s32[]{:S(2)}) async-start(), calls=%async_computation.13 | async-start | bytes 34603008 | tf_op jit(solution)/shard_map/reduce_scatter | solution.py:305
  1747.5 1592.1 %copy-start.1 = (bf16[1,768,2048]{2,1,0:T(8,128)(2,1)S(1)}, bf16[1,768,2048]{2,1,0:T(8,128)(2,1)}, u32[]{:S(2)}) copy-start(bf16[1,768,2048]{2,1,0:T(8,128)(2,1)} %param.27) | copy-start | bytes 9437188
  (86 other events, 872.0 us)
Sparse Core Ops, SparseCore 0:
  11.0 59.5 all-gather.5
  73.6 55.3 all-gather.7
  132.0 113.7 all-gather.9
  248.6 113.0 all-gather.11
  1357.0 191.1 reduce-scatter.15
  1607.3 154.7 reduce-scatter.11
  1765.1 146.4 reduce-scatter.9
  1914.6 710.7 reduce-scatter.13
  2628.3 711.2 reduce-scatter.7
where the time goes:
time: 3360 us; the launch traced here: 3350 us
  waiting for transfers between devices  2320 us (69%)
  blocking collectives  383 us (11%)
  matrix products  246 us (7%)
  other arithmetic  178 us (5%)
  local copies, waits for them, and re-layouts  173 us (5%)
    reduce_scatter x1, waiting for transfers between devices, local(): lax.psum_scatter(grad_terms[0], ('expert', 'fsdp'), scatter_dimension=0,...  714 us
    reduce_scatter x1, waiting for transfers between devices, local(): lax.psum_scatter(grad_terms[3], ('expert', 'fsdp'), scatter_dimension=0,...  714 us
    all_gather x1, blocking collectives, local(): lax.all_gather(w_router, ('expert', 'fsdp'), axis=0, tiled=True)  293 us
    all_to_all x1, waiting for transfers between devices, send_grads(): lax.all_to_all(buffer, ('expert', 'fsdp'), split_axis=0, concat_axis=0, t...  199 us
    all_to_all x1, waiting for transfers between devices, return_rows(): lax.all_to_all(buffer, ('expert', 'fsdp'), split_axis=0, concat_axis=0, t...  196 us
    all_to_all x1, waiting for transfers between devices, return_grads(): lax.all_to_all(buffer, ('expert', 'fsdp'), split_axis=0, concat_axis=0, t...  160 us
    reduce_scatter x1, waiting for transfers between devices, local(): lax.psum_scatter(grad_terms[1], ('expert', 'fsdp'), scatter_dimension=0,...  107 us
    all_gather x1, waiting for transfers between devices, local(): lax.all_gather(w_query, ('expert', 'fsdp'), axis=0, tiled=True)  106 us
  transfers between devices with their start and end apart: 13, of which 9 were waited for; matrix products, arithmetic and copies ran while one was open for 15% of the time, Pallas kernels for 0%

commit v1 on v0

v1 whole, which is shorter than its diff:
```python
from functools import partial

import jax
import jax.numpy as jnp
from jax import lax
from jax.experimental import pallas as pl
from jax.experimental.pallas import tpu as pltpu
from jax.sharding import PartitionSpec as P

EPSILON = 1e-06
MESH = pl.DeviceIdType.MESH
BF = jnp.bfloat16
F32 = jnp.float32
HEAD = 128
ANY = pl.BlockSpec(memory_space=pl.ANY)
VM = pl.BlockSpec(memory_space=pltpu.VMEM)
DMA = pltpu.SemaphoreType.DMA
BIG = 60 * 1024 * 1024


def dot(a, b):
    return lax.dot_general(a, b, (((1,), (0,)), ((), ())), preferred_element_type=F32)


def dot_last(a, b):
    return lax.dot_general(a, b, (((1,), (1,)), ((), ())), preferred_element_type=F32)


def dot_first(a, b):
    return lax.dot_general(a, b, (((0,), (0,)), ((), ())), preferred_element_type=F32)


def place():
    return lax.axis_index("expert"), lax.axis_index("fsdp")


def remote(src, dst, send, recv, where):
    return pltpu.make_async_remote_copy(
        src_ref=src,
        dst_ref=dst,
        send_sem=send,
        recv_sem=recv,
        device_id=where,
        device_id_type=MESH,
    )


def near(z, k, n_z):
    sign = 1 - 2 * (z // (n_z // 2))
    return lax.rem(z + sign * k + n_z, n_z)


def greet_all(n_e, n_z):
    e, z = place()
    me, n = e * n_z + z, n_e * n_z
    barrier = pltpu.get_barrier_semaphore()

    @pl.loop(1, n)
    def _(k):
        other = lax.rem(me + k, n)
        pl.semaphore_signal(
            barrier,
            inc=1,
            device_id=(other // n_z, lax.rem(other, n_z)),
            device_id_type=MESH,
        )

    pl.semaphore_wait(barrier, n - 1)


def greet(n_e, n_z, along_z):
    e, z = place()
    barrier = pltpu.get_barrier_semaphore()
    for k in range(1, n_e):
        pl.semaphore_signal(
            barrier, inc=1, device_id=(lax.rem(e + k, n_e), z), device_id_type=MESH
        )
    count = n_e - 1
    if along_z:
        for k in range(1, n_z):
            pl.semaphore_signal(
                barrier, inc=1, device_id=(e, lax.rem(z + k, n_z)), device_id_type=MESH
            )
        count += n_z - 1
    pl.semaphore_wait(barrier, count)


def ranked(z, k, n_z):
    half = n_z // 2
    top = z // half
    low = z + top * (n_z - 1 - 2 * z)
    at = k - low * jnp.where(k == 1, 1, 0)
    return at + top * (n_z - 1 - 2 * at)


def partner_chip(chip, k):
    low = lax.rem(lax.rem(chip, 2) + lax.rem(k, 2), 2)
    high = lax.rem(chip // 2 + k // 2, 2)
    return 2 * high + low


def chain_start(n_z, src, dst_at, send, recv):
    e, z = place()

    @pl.when(z + 1 < n_z)
    def _():
        remote(src, dst_at(z), send.at[0], recv.at[z], (e, z + 1)).start()

    @pl.when(z > 0)
    def _():
        remote(src, dst_at(z), send.at[1], recv.at[z], (e, z - 1)).start()


def chain_take(n_z, k, dst_at, send, recv):
    e, z = place()
    sz = ranked(z, k, n_z)
    block = dst_at(sz)
    step = jnp.where(sz < z, 1, -1)
    remote(block, block, send.at[1 + k], recv.at[sz], (e, sz)).wait_recv()

    @pl.when((z + step >= 0) & (z + step < n_z))
    def _():
        remote(block, block, send.at[1 + k], recv.at[sz], (e, z + step)).start()

    return sz


def chain_end(n_z, src, dst_at, send, recv):
    e, z = place()

    @pl.when(z + 1 < n_z)
    def _():
        remote(src, dst_at(z), send.at[0], recv.at[z], (e, z + 1)).wait_send()

    @pl.when(z > 0)
    def _():
        remote(src, dst_at(z), send.at[1], recv.at[z], (e, z - 1)).wait_send()

    for k in range(1, n_z):
        sz = ranked(z, k, n_z)
        step = jnp.where(sz < z, 1, -1)

        @pl.when((z + step >= 0) & (z + step < n_z))
        def _(k=k, sz=sz, step=step):
            block = dst_at(sz)
            remote(block, block, send.at[1 + k], recv.at[sz], (e, z + step)).wait_send()


def plane_gather_start(n_e, x_ref, out_ref, own, send, recv, sib_send, sib_recv):
    e, z = place()
    nc, chip, core = n_e // 2, e // 2, lax.rem(e, 2)
    pltpu.make_async_copy(x_ref, out_ref.at[e], own).start()
    for k in range(1, nc):
        j = lax.rem(chip + k, nc)
        remote(
            x_ref, out_ref.at[e], send.at[k], recv.at[chip], (2 * j + core, z)
        ).start()
    remote(
        x_ref, out_ref.at[e], sib_send.at[0], sib_recv.at[chip], (2 * chip + 1 - core, z)
    ).start()


def plane_gather_end(n_e, x_ref, out_ref, own, send, recv, sib_send, sib_recv):
    e, z = place()
    nc, chip, core = n_e // 2, e // 2, lax.rem(e, 2)
    sib = (2 * chip + 1 - core, z)
    for k in range(1, nc):
        j = lax.rem(chip + nc - k, nc)
        block = out_ref.at[2 * j + core]
        remote(x_ref, block, send.at[k], recv.at[j], (2 * j + core, z)).wait()
        remote(block, block, sib_send.at[k], sib_recv.at[j], sib).start()
    for k in range(nc):
        j = lax.rem(chip + nc - k, nc)
        block = out_ref.at[2 * j + 1 - core]
        remote(x_ref, block, sib_send.at[k], sib_recv.at[j], sib).wait()
    pltpu.make_async_copy(x_ref, out_ref.at[e], own).wait()


def share_kernel(
    n_e,
    n_z,
    x_ref,
    ct_ref,
    rt_ref,
    wq_ref,
    wo_ref,
    mi_ref,
    xs_ref,
    cts_ref,
    rts_ref,
    wqs_ref,
    wos_ref,
    mis_ref,
    own,
    x_send,
    x_recv,
    sib_send,
    sib_recv,
    z_send,
    z_recv,
    a_send,
    a_recv,
):
    e, z = place()
    n, me = n_e * n_z, e * n_z + z
    greet_all(n_e, n_z)
    gather = (n_e, x_ref, xs_ref, own.at[0], x_send, x_recv, sib_send, sib_recv)
    plane_gather_start(*gather)

    def other_of(k):
        other = lax.rem(me + k, n)
        return other, other // n_z, lax.rem(other, n_z)

    @pl.loop(1, n)
    def _(k):
        other, oe, oz = other_of(k)
        remote(
            wq_ref.at[oe], wqs_ref.at[me], a_send.at[0, k], a_recv.at[0, me], (oe, oz)
        ).start()
        remote(
            mi_ref, mis_ref.at[me], a_send.at[1, k], a_recv.at[1, me], (oe, oz)
        ).start()

    along = ((rt_ref, rts_ref), (wo_ref, wos_ref), (ct_ref, cts_ref))
    for i, (src, dst) in enumerate(along):
        for k in range(1, n_z):
            oz = near(z, k, n_z)
            remote(src, dst.at[z], z_send.at[i, k], z_recv.at[i, z], (e, oz)).start()
        pltpu.make_async_copy(src, dst.at[z], own.at[1 + i]).start()
    pltpu.make_async_copy(wq_ref.at[e], wqs_ref.at[me], own.at[4]).start()
    pltpu.make_async_copy(mi_ref, mis_ref.at[me], own.at[5]).start()

    plane_gather_end(*gather)

    @pl.loop(1, n)
    def _(k):
        other, oe, oz = other_of(k)
        remote(
            wq_ref.at[oe],
            wqs_ref.at[other],
            a_send.at[0, k],
            a_recv.at[0, other],
            (oe, oz),
        ).wait()
        remote(
            mi_ref, mis_ref.at[other], a_send.at[1, k], a_recv.at[1, other], (oe, oz)
        ).wait()

    for i, (src, dst) in enumerate(along):
        for k in range(1, n_z):
            oz = near(z, k, n_z)
            remote(src, dst.at[oz], z_send.at[i, k], z_recv.at[i, oz], (e, oz)).wait()
        pltpu.make_async_copy(src, dst.at[z], own.at[1 + i]).wait()
    pltpu.make_async_copy(wq_ref.at[e], wqs_ref.at[me], own.at[4]).wait()
    pltpu.make_async_copy(mi_ref, mis_ref.at[me], own.at[5]).wait()


def share(n_e, n_z, tokens, cotangent, routes, wq, wo, misc):
    n, nc = n_e * n_z, n_e // 2

    def like(lead, a):
        return jax.ShapeDtypeStruct((lead,) + a.shape, a.dtype)

    return pl.pallas_call(
        partial(share_kernel, n_e, n_z),
        out_shape=(
            like(n_e, tokens),
            like(n_z, cotangent),
            like(n_z, routes),
            like(n, wq[0]),
            like(n_z, wo),
            like(n, misc),
        ),
        in_specs=[ANY] * 6,
        out_specs=(ANY,) * 6,
        scratch_shapes=[
            DMA((6,)),
            DMA((nc,)),
            DMA((nc,)),
            DMA((nc,)),
            DMA((nc,)),
            DMA((3, n_z)),
            DMA((3, n_z)),
            DMA((2, n)),
            DMA((2, n)),
        ],
        compiler_params=pltpu.CompilerParams(collective_id=1, has_side_effects=True),
        name="share",
    )(tokens, cotangent, routes, wq, wo, misc)


def plane_sum_body(
    n_e, part_ref, total_ref, mine, sib, far, own, send, recv, sib_send, sib_recv
):
    e, z = place()
    nc, chip, core = n_e // 2, e // 2, lax.rem(e, 2)
    rows = total_ref.shape[0]
    step = 32
    other = (2 * chip + 1 - core, z)
    for k in range(nc):
        j = lax.rem(chip + 1 + k, nc)
        remote(
            part_ref.at[2 * j + 1 - core],
            sib.at[j],
            sib_send.at[j],
            sib_recv.at[j],
            other,
        ).start()
        pltpu.make_async_copy(part_ref.at[2 * j + core], mine.at[j], own.at[j]).start()
    for k in range(nc):
        j = lax.rem(chip + 1 + k, nc)
        remote(
            part_ref.at[2 * j + 1 - core],
            sib.at[j],
            sib_send.at[j],
            sib_recv.at[j],
            other,
        ).wait()
        pltpu.make_async_copy(part_ref.at[2 * j + core], mine.at[j], own.at[j]).wait()
        if k < nc - 1:

            @pl.loop(0, rows, step=step)
            def _(r, j=j):
                at = pl.ds(pl.multiple_of(r, step), step)
                mine[j, at, :] = (
                    mine[j, at, :].astype(F32) + sib[j, at, :].astype(F32)
                ).astype(BF)

            remote(
                mine.at[j], far.at[chip], send.at[j], recv.at[chip], (2 * j + core, z)
            ).start()
        else:

            @pl.loop(0, rows, step=step)
            def _(r, j=j):
                at = pl.ds(pl.multiple_of(r, step), step)
                total_ref[at, :] = mine[j, at, :].astype(F32) + sib[j, at, :].astype(F32)

    for k in range(1, nc):
        j = lax.rem(chip + nc - k, nc)
        remote(
            mine.at[j], far.at[j], send.at[j], recv.at[j], (2 * j + core, z)
        ).wait()

        @pl.loop(0, rows, step=step)
        def _(r, j=j):
            at = pl.ds(pl.multiple_of(r, step), step)
            total_ref[at, :] += far[j, at, :].astype(F32)


def plane_sum_scratch(n_e, part):
    nc = n_e // 2
    block = (nc,) + part.shape[1:]
    return [pltpu.VMEM(block, BF)] * 3 + [DMA((nc,))] * 5


def plane_sum_kernel(n_e, n_z, part_ref, total_ref, *scratch):
    greet(n_e, n_z, False)
    plane_sum_body(n_e, part_ref, total_ref, *scratch)


def plane_sum(n_e, n_z, part):
    return pl.pallas_call(
        partial(plane_sum_kernel, n_e, n_z),
        out_shape=jax.ShapeDtypeStruct(part.shape[1:], F32),
        in_specs=[ANY],
        out_specs=VM,
        scratch_shapes=plane_sum_scratch(n_e, part),
        compiler_params=pltpu.CompilerParams(
            collective_id=2, has_side_effects=True, vmem_limit_bytes=BIG
        ),
        name="plane_sum",
    )(part)


def plane_gather_kernel(n_e, n_z, x_ref, out_ref, *sems):
    greet(n_e, n_z, False)
    plane_gather_start(n_e, x_ref, out_ref, *sems)
    plane_gather_end(n_e, x_ref, out_ref, *sems)


def plane_gather(n_e, n_z, x):
    nc = n_e // 2
    return pl.pallas_call(
        partial(plane_gather_kernel, n_e, n_z),
        out_shape=jax.ShapeDtypeStruct((n_e,) + x.shape, x.dtype),
        in_specs=[ANY],
        out_specs=ANY,
        scratch_shapes=[DMA] + [DMA((nc,))] * 4,
        compiler_params=pltpu.CompilerParams(collective_id=3, has_side_effects=True),
        name="plane_gather",
    )(x)


def pieces(columns, wide=512):
    cuts = list(range(0, columns - columns % wide, wide)) + [columns - columns % wide]
    spans = [(a, b - a) for a, b in zip(cuts, cuts[1:])]
    if columns % wide:
        spans.append((cuts[-1], columns % wide))
    return spans


def rows_out(n_e, cap, k, sz, src, d_ref, rows, out_ref, own, send, recv):
    e, z = place()
    pick = d_ref[sz]
    for start, size in pieces(src.shape[-1]):
        rows[k, :, start : start + size] = dot(pick, src[:, start : start + size]).astype(BF)
    for i in range(1, n_e + 1):
        oe = lax.rem(e + i, n_e)
        block = rows.at[k, pl.ds(pl.multiple_of(oe * cap, 16), cap), :]
        if i < n_e:
            remote(block, out_ref.at[sz, e], send.at[k, i], recv.at[sz, e], (oe, z)).start()
        else:
            pltpu.make_async_copy(block, out_ref.at[sz, e], own.at[k]).start()


def rows_out_wait(n_e, cap, k, sz, rows, out_ref, own, send, recv):
    e, z = place()
    for i in range(1, n_e + 1):
        oe = lax.rem(e + i, n_e)
        at = pl.ds(pl.multiple_of(oe * cap, 16), cap)
        block = rows.at[k, at, :]
        if i < n_e:
            remote(
                block, out_ref.at[sz, oe], send.at[k, i], recv.at[sz, oe], (oe, z)
            ).wait()
        else:
            pltpu.make_async_copy(block, out_ref.at[sz, e], own.at[k]).wait()


def open_kernel(
    n_e,
    n_z,
    cap,
    x_ref,
    ct_ref,
    rt_ref,
    wq_ref,
    wo_ref,
    mi_ref,
    pick_ref,
    xs_ref,
    rts_ref,
    wqs_ref,
    wos_ref,
    mis_ref,
    dy_ref,
    rows,
    own,
    x_send,
    x_recv,
    sib_send,
    sib_recv,
    w_send,
    w_recv,
    zw_send,
    zw_recv,
    zo_send,
    zo_recv,
    zr_send,
    zr_recv,
    m_send,
    m_recv,
    r_send,
    r_recv,
):
    e, z = place()
    n, me = n_e * n_z, e * n_z + z
    greet_all(n_e, n_z)

    def plane_peer(i):
        return lax.rem(e + i, n_e)

    for i in range(1, n_e):
        oe = plane_peer(i)
        remote(
            wq_ref.at[oe], wqs_ref.at[e, z], w_send.at[i], w_recv.at[e], (oe, z)
        ).start()
    kept = (
        (wq_ref.at[e], wqs_ref.at[e, z]),
        (wo_ref, wos_ref.at[z]),
        (rt_ref, rts_ref.at[z]),
        (mi_ref, mis_ref.at[me]),
    )
    for i, (src, dst) in enumerate(kept):
        pltpu.make_async_copy(src, dst, own.at[i]).start()
    out_chain = (lambda s: wos_ref.at[s], zo_send, zo_recv)
    chain_start(n_z, wo_ref, *out_chain)
    for k in range(1, n_z):
        oz = near(z, k, n_z)
        remote(rt_ref, rts_ref.at[z], zr_send.at[k], zr_recv.at[z], (e, oz)).start()

    def other_of(k):
        other = lax.rem(me + k, n)
        return other, (other // n_z, lax.rem(other, n_z))

    @pl.loop(1, n)
    def _(k):
        other, where = other_of(k)
        remote(mi_ref, mis_ref.at[me], m_send.at[k], m_recv.at[me], where).start()

    gather = (n_e, x_ref, xs_ref, own.at[4], x_send, x_recv, sib_send, sib_recv)
    plane_gather_start(*gather)
    pick = pick_ref[...]
    for start, size in pieces(ct_ref.shape[-1]):
        rows[:, start : start + size] = dot(pick, ct_ref[:, start : start + size]).astype(BF)
    for i in range(1, n_e + 1):
        oe = plane_peer(i)
        block = rows.at[pl.ds(pl.multiple_of(oe * cap, 16), cap), :]
        if i < n_e:
            remote(block, dy_ref.at[e], r_send.at[i], r_recv.at[e], (oe, z)).start()
        else:
            pltpu.make_async_copy(block, dy_ref.at[e], own.at[5]).start()

    for i in range(1, n_e):
        oe = plane_peer(i)
        remote(
            wq_ref.at[oe], wqs_ref.at[oe, z], w_send.at[i], w_recv.at[oe], (oe, z)
        ).wait()
    pltpu.make_async_copy(*kept[0], own.at[0]).wait()
    in_chain = (lambda s: wqs_ref.at[:, s], zw_send, zw_recv)
    chain_start(n_z, wqs_ref.at[:, z], *in_chain)
    for k in range(1, n_z):
        chain_take(n_z, k, *out_chain)
        chain_take(n_z, k, *in_chain)
        if k == n_z - 2:
            plane_gather_end(*gather)
    chain_end(n_z, wo_ref, *out_chain)
    chain_end(n_z, wqs_ref.at[:, z], *in_chain)
    for k in range(1, n_z):
        oz = near(z, k, n_z)
        remote(rt_ref, rts_ref.at[oz], zr_send.at[k], zr_recv.at[oz], (e, oz)).wait()

    @pl.loop(1, n)
    def _(k):
        other, where = other_of(k)
        remote(mi_ref, mis_ref.at[other], m_send.at[k], m_recv.at[other], where).wait()

    for i in range(1, n_e + 1):
        oe = plane_peer(i)
        block = rows.at[pl.ds(pl.multiple_of(oe * cap, 16), cap), :]
        if i < n_e:
            remote(block, dy_ref.at[oe], r_send.at[i], r_recv.at[oe], (oe, z)).wait()
        else:
            pltpu.make_async_copy(block, dy_ref.at[e], own.at[5]).wait()
    for i, (src, dst) in enumerate(kept):
        if i:
            pltpu.make_async_copy(src, dst, own.at[i]).wait()


def open_layer(n_e, n_z, cap, tokens, cotangent, routes, wq, wo, misc, pick):
    n, nc = n_e * n_z, n_e // 2
    _, shard, columns = wq.shape
    width = tokens.shape[1]

    def like(lead, a):
        return jax.ShapeDtypeStruct((lead,) + a.shape, a.dtype)

    return pl.pallas_call(
        partial(open_kernel, n_e, n_z, cap),
        out_shape=(
            like(n_e, tokens),
            like(n_z, routes),
            jax.ShapeDtypeStruct((n_e, n_z, shard, columns), BF),
            like(n_z, wo),
            like(n, misc),
            jax.ShapeDtypeStruct((n_e, cap, width), BF),
        ),
        in_specs=[ANY, VM] + [ANY] * 4 + [VM],
        out_specs=(ANY,) * 6,
        scratch_shapes=[
            pltpu.VMEM((n_e * cap, width), BF),
            DMA((6,)),
            DMA((nc,)),
            DMA((nc,)),
            DMA((nc,)),
            DMA((nc,)),
            DMA((n_e,)),
            DMA((n_e,)),
            DMA((n_z + 1,)),
            DMA((n_z,)),
            DMA((n_z + 1,)),
            DMA((n_z,)),
            DMA((n_z,)),
            DMA((n_z,)),
            DMA((n,)),
            DMA((n,)),
            DMA((n_e,)),
            DMA((n_e,)),
        ],
        compiler_params=pltpu.CompilerParams(
            collective_id=11, has_side_effects=True, vmem_limit_bytes=BIG
        ),
        name="open_layer",
    )(tokens, cotangent, routes, wq, wo, misc, pick)


def dispatch_kernel(
    n_e,
    n_z,
    cap,
    tok_ref,
    d_ref,
    out_ref,
    zbuf,
    rows,
    own,
    z_send,
    z_recv,
    send,
    recv,
):
    e, z = place()
    greet(n_e, n_z, True)
    chain = (lambda s: zbuf.at[s], z_send, z_recv)
    chain_start(n_z, tok_ref, *chain)
    for k in range(n_z):
        sz = chain_take(n_z, k, *chain) if k else z
        src = zbuf.at[sz] if k else tok_ref
        rows_out(n_e, cap, k, sz, src, d_ref, rows, out_ref, own, send, recv)
    for k in range(n_z):
        sz = ranked(z, k, n_z) if k else z
        rows_out_wait(n_e, cap, k, sz, rows, out_ref, own, send, recv)
    chain_end(n_z, tok_ref, *chain)


def dispatch(n_e, n_z, cap, tok, picks):
    count, columns = tok.shape
    return pl.pallas_call(
        partial(dispatch_kernel, n_e, n_z, cap),
        out_shape=jax.ShapeDtypeStruct((n_z, n_e, cap, columns), BF),
        in_specs=[VM, VM],
        out_specs=ANY,
        scratch_shapes=[
            pltpu.VMEM((n_z, count, columns), BF),
            pltpu.VMEM((n_z, n_e * cap, columns), BF),
            DMA((n_z,)),
            DMA((n_z + 1,)),
            DMA((n_z,)),
            DMA((n_z, n_e)),
            DMA((n_z, n_e)),
        ],
        compiler_params=pltpu.CompilerParams(
            collective_id=4, has_side_effects=True, vmem_limit_bytes=BIG
        ),
        name="dispatch",
    )(tok, picks)


def send_kernel(n_e, n_z, cap, src_ref, d_ref, out_ref, rows, own, send, recv):
    e, z = place()
    greet(n_e, n_z, False)
    for k in range(n_z):
        sz = near(z, k, n_z)
        rows_out(n_e, cap, k, sz, src_ref.at[sz], d_ref, rows, out_ref, own, send, recv)
    for k in range(n_z):
        rows_out_wait(n_e, cap, k, near(z, k, n_z), rows, out_ref, own, send, recv)


def send_rows(n_e, n_z, cap, src, picks):
    columns = src.shape[-1]
    return pl.pallas_call(
        partial(send_kernel, n_e, n_z, cap),
        out_shape=jax.ShapeDtypeStruct((n_z, n_e, cap, columns), BF),
        in_specs=[VM, VM],
        out_specs=ANY,
        scratch_shapes=[
            pltpu.VMEM((n_z, n_e * cap, columns), BF),
            DMA((n_z,)),
            DMA((n_z, n_e)),
            DMA((n_z, n_e)),
        ],
        compiler_params=pltpu.CompilerParams(
            collective_id=5, has_side_effects=True, vmem_limit_bytes=BIG
        ),
        name="send_rows",
    )(src, picks)


def give_back_kernel(
    n_e,
    n_z,
    cap,
    y_ref,
    d_ref,
    out_ref,
    rbuf,
    pbuf,
    own,
    send,
    recv,
    z_own,
    z_send,
    z_recv,
):
    e, z = place()
    greet(n_e, n_z, True)
    order = list(range(n_z - 1, -1, -1))
    for k in order:
        sz = near(z, k, n_z)
        for i in range(1, n_e + 1):
            oe = lax.rem(e + i, n_e)
            if i < n_e:
                remote(
                    y_ref.at[sz, oe],
                    rbuf.at[sz, e],
                    send.at[k, i],
                    recv.at[sz, e],
                    (oe, z),
                ).start()
            else:
                pltpu.make_async_copy(y_ref.at[sz, e], rbuf.at[sz, e], own.at[k]).start()
    for k in order:
        sz = near(z, k, n_z)
        for i in range(1, n_e + 1):
            oe = lax.rem(e + i, n_e)
            if i < n_e:
                remote(
                    y_ref.at[sz, oe],
                    rbuf.at[sz, oe],
                    send.at[k, i],
                    recv.at[sz, oe],
                    (oe, z),
                ).wait()
            else:
                pltpu.make_async_copy(y_ref.at[sz, e], rbuf.at[sz, e], own.at[k]).wait()
        pick = d_ref[sz]
        for start, size in pieces(pbuf.shape[-1]):
            block = rbuf[sz, :, :, start : start + size].reshape(n_e * cap, size)
            pbuf[k, :, start : start + size] = dot(pick, block).astype(BF)
        if k:
            remote(
                pbuf.at[k], out_ref.at[z], z_send.at[k], z_recv.at[z], (e, sz)
            ).start()
        else:
            pltpu.make_async_copy(pbuf.at[k], out_ref.at[z], z_own).start()
    for k in order:
        sz = near(z, k, n_z)
        if k:
            remote(
                pbuf.at[k], out_ref.at[sz], z_send.at[k], z_recv.at[sz], (e, sz)
            ).wait()
        else:
            pltpu.make_async_copy(pbuf.at[k], out_ref.at[z], z_own).wait()


def give_back(n_e, n_z, cap, y, picks, number):
    columns = y.shape[-1]
    count = picks.shape[1]
    return pl.pallas_call(
        partial(give_back_kernel, n_e, n_z, cap),
        out_shape=jax.ShapeDtypeStruct((n_z, count, columns), BF),
        in_specs=[ANY, VM],
        out_specs=ANY,
        scratch_shapes=[
            pltpu.VMEM((n_z, n_e, cap, columns), BF),
            pltpu.VMEM((n_z, count, columns), BF),
            DMA((n_z,)),
            DMA((n_z, n_e)),
            DMA((n_z, n_e)),
            DMA,
            DMA((n_z,)),
            DMA((n_z,)),
        ],
        compiler_params=pltpu.CompilerParams(
            collective_id=number, has_side_effects=True, vmem_limit_bytes=BIG
        ),
        name="give_back",
    )(y, picks)


def finish_kernel(
    n_e,
    n_z,
    part_ref,
    gw_ref,
    go_ref,
    gm_ref,
    total_ref,
    gws_ref,
    gos_ref,
    gms_ref,
    own_g,
    a_send,
    a_recv,
    z_send,
    z_recv,
    *scratch,
):
    e, z = place()
    n, me = n_e * n_z, e * n_z + z
    greet_all(n_e, n_z)

    def other_of(k):
        other = lax.rem(me + k, n)
        return other, (other // n_z, lax.rem(other, n_z))

    @pl.loop(1, n)
    def _(k):
        other, where = other_of(k)
        remote(
            gw_ref.at[other], gws_ref.at[me], a_send.at[0, k], a_recv.at[0, me], where
        ).start()
        remote(
            gm_ref.at[other], gms_ref.at[me], a_send.at[1, k], a_recv.at[1, me], where
        ).start()

    for k in range(1, n_z):
        oz = near(z, k, n_z)
        remote(
            go_ref.at[oz], gos_ref.at[z], z_send.at[k], z_recv.at[z], (e, oz)
        ).start()
    mine = (
        (gw_ref.at[me], gws_ref.at[me]),
        (gm_ref.at[me], gms_ref.at[me]),
        (go_ref.at[z], gos_ref.at[z]),
    )
    for i, (src, dst) in enumerate(mine):
        pltpu.make_async_copy(src, dst, own_g.at[i]).start()

    plane_sum_body(n_e, part_ref, total_ref, *scratch)

    @pl.loop(1, n)
    def _(k):
        other, where = other_of(k)
        remote(
            gw_ref.at[other],
            gws_ref.at[other],
            a_send.at[0, k],
            a_recv.at[0, other],
            where,
        ).wait()
        remote(
            gm_ref.at[other],
            gms_ref.at[other],
            a_send.at[1, k],
            a_recv.at[1, other],
            where,
        ).wait()

    for k in range(1, n_z):
        oz = near(z, k, n_z)
        remote(
            go_ref.at[oz], gos_ref.at[oz], z_send.at[k], z_recv.at[oz], (e, oz)
        ).wait()
    for i, (src, dst) in enumerate(mine):
        pltpu.make_async_copy(src, dst, own_g.at[i]).wait()


def finish(n_e, n_z, part, gw, go, gm):
    n = n_e * n_z
    return pl.pallas_call(
        partial(finish_kernel, n_e, n_z),
        out_shape=(
            jax.ShapeDtypeStruct(part.shape[1:], F32),
            jax.ShapeDtypeStruct(gw.shape, gw.dtype),
            jax.ShapeDtypeStruct(go.shape, go.dtype),
            jax.ShapeDtypeStruct(gm.shape, gm.dtype),
        ),
        in_specs=[ANY] * 4,
        out_specs=(VM, ANY, ANY, ANY),
        scratch_shapes=[
            DMA((3,)),
            DMA((2, n)),
            DMA((2, n)),
            DMA((n_z,)),
            DMA((n_z,)),
        ]
        + plane_sum_scratch(n_e, part),
        compiler_params=pltpu.CompilerParams(
            collective_id=8, has_side_effects=True, vmem_limit_bytes=BIG
        ),
        name="finish",
    )(part, gw, go, gm)


def head_norm(u, gain):
    r = lax.rsqrt(jnp.mean(u * u, axis=-1, keepdims=True) + EPSILON)
    return u * r * gain


def turn(u, cos, sin):
    return u * cos + pltpu.roll(u, HEAD // 2, 1) * sin


def turn_back(u, cos, sin):
    return u * cos - pltpu.roll(u, HEAD // 2, 1) * sin


def turns(table):
    other = pltpu.roll(table, HEAD // 2, 1)
    first = lax.broadcasted_iota(jnp.int32, table.shape, 1) < HEAD // 2
    return jnp.where(first, table, other), jnp.where(first, -other, table)


def may_see(seg_row):
    count = seg_row.shape[1]
    i = lax.broadcasted_iota(jnp.int32, (count, count), 0)
    j = lax.broadcasted_iota(jnp.int32, (count, count), 1)
    seg_col = jnp.sum(jnp.where(i == j, seg_row, 0.0), axis=1, keepdims=True)
    return ((seg_col == seg_row) & (seg_col >= 0) & (j <= i)) | (i == j)


def probabilities(q, k, allowed):
    scores = jnp.where(allowed, dot_last(q, k) * (HEAD**-0.5), -1e30)
    peak = jnp.max(scores, axis=-1, keepdims=True)
    weight = jnp.exp(scores - peak)
    return weight / jnp.sum(weight, axis=-1, keepdims=True)


def attend_block(
    heads, x, cos, sin, allowed, w_ref, wo_ref, g1_ref, gh_ref, n1_ref, raw_ref, v_ref, mix_ref
):
    x = x.astype(F32)
    r = lax.rsqrt(jnp.mean(x * x, axis=-1, keepdims=True) + EPSILON)
    n1 = (x * r * g1_ref[...]).astype(BF)
    n1_ref[...] = n1
    raw = dot(n1, w_ref[...])
    qk = (heads + 1) * HEAD
    raw_ref[...] = raw[:, :qk]
    value = raw[:, qk:].astype(BF)
    v_ref[...] = value
    gq, gk = gh_ref[0:1, :], gh_ref[1:2, :]
    key = turn(head_norm(raw[:, heads * HEAD : qk], gk), cos, sin).astype(BF)
    for h in range(heads):
        at = slice(h * HEAD, (h + 1) * HEAD)
        query = turn(head_norm(raw[:, at], gq), cos, sin).astype(BF)
        weight = probabilities(query, key, allowed).astype(BF)
        mix_ref[:, at] = dot(weight, value).astype(BF)
    return dot(mix_ref[...], wo_ref[...]).astype(BF)


def attend_kernel(
    heads,
    x_ref,
    turn_ref,
    seg_ref,
    w_ref,
    wo_ref,
    g1_ref,
    gh_ref,
    n1_ref,
    raw_ref,
    v_ref,
    mix_ref,
    part_ref,
):
    part_ref[0] = attend_block(
        heads,
        x_ref[0],
        *turns(turn_ref[0]),
        may_see(seg_ref[0]),
        w_ref,
        wo_ref,
        g1_ref,
        gh_ref,
        n1_ref.at[0],
        raw_ref.at[0],
        v_ref.at[0],
        mix_ref.at[0],
    )


def attend(n_e, heads, xs, turn_table, seg, w, wo, g1, gh):
    _, count, width = xs.shape

    def block(*shape):
        return pl.BlockSpec((1,) + shape, lambda b: (b, 0, 0))

    def whole(*shape):
        return pl.BlockSpec(shape, lambda b: (0, 0))

    outs = ((width, BF), ((heads + 1) * HEAD, F32), (HEAD, BF), (heads * HEAD, BF), (width, BF))
    return pl.pallas_call(
        partial(attend_kernel, heads),
        grid=(n_e,),
        out_shape=tuple(jax.ShapeDtypeStruct((n_e, count, c), t) for c, t in outs),
        in_specs=[
            block(count, width),
            block(count, HEAD),
            block(1, count),
            whole(*w.shape),
            whole(*wo.shape),
            whole(*g1.shape),
            whole(*gh.shape),
        ],
        out_specs=tuple(block(count, c) for c, _ in outs),
        compiler_params=pltpu.CompilerParams(vmem_limit_bytes=BIG),
        name="attend",
    )(xs, turn_table, seg, w, wo, g1, gh)


def front_kernel(
    n_e,
    n_z,
    cap,
    heads,
    xs_ref,
    ct_ref,
    pick_ref,
    turn_ref,
    seg_ref,
    w_ref,
    wo_ref,
    g1_ref,
    gh_ref,
    n1_ref,
    raw_ref,
    v_ref,
    mix_ref,
    total_ref,
    dy_ref,
    xbuf,
    n1buf,
    rawbuf,
    vbuf,
    mixbuf,
    away,
    mine,
    sib,
    far,
    zbuf,
    rows,
    x_sem,
    o_sem,
    sib_send,
    sib_recv,
    send,
    recv,
    z_send,
    z_recv,
    r_send,
    r_recv,
    r_own,
):
    e, z = place()
    nc, chip, core = n_e // 2, e // 2, lax.rem(e, 2)
    sibling = (2 * chip + 1 - core, z)
    count = total_ref.shape[0]
    step = 32
    greet(n_e, n_z, True)
    chain = (lambda s: zbuf.at[s], z_send, z_recv)
    chain_start(n_z, ct_ref, *chain)

    def blocks(k):
        j = partner_chip(chip, nc - 1 - k)
        return j, (2 * j + 1 - core, 2 * j + core)

    def load(b, slot):
        return pltpu.make_async_copy(xs_ref.at[b], xbuf.at[slot], x_sem.at[slot])

    def stores(b, slot):
        pairs = ((n1buf, n1_ref), (rawbuf, raw_ref), (vbuf, v_ref), (mixbuf, mix_ref))
        return [
            pltpu.make_async_copy(src.at[slot], dst.at[b], o_sem.at[i, slot])
            for i, (src, dst) in enumerate(pairs)
        ]

    for slot in range(2):
        load(blocks(0)[1][slot], slot).start()

    @pl.loop(0, nc)
    def _(k):
        j, pair = blocks(k)
        for slot, b in enumerate(pair):
            load(b, slot).wait()

            @pl.when(k > 0)
            def _(b=b, slot=slot):
                for copy in stores(b, slot):
                    copy.wait()

            part = attend_block(
                heads,
                xbuf[slot],
                *turns(turn_ref[b]),
                may_see(seg_ref[b]),
                w_ref,
                wo_ref,
                g1_ref,
                gh_ref,
                n1buf.at[slot],
                rawbuf.at[slot],
                vbuf.at[slot],
                mixbuf.at[slot],
            )
            for copy in stores(b, slot):
                copy.start()

            @pl.when(k < nc - 1)
            def _(slot=slot):
                load(blocks(k + 1)[1][slot], slot).start()

            if slot == 0:
                away[j] = part
                remote(
                    away.at[j], sib.at[j], sib_send.at[j], sib_recv.at[j], sibling
                ).start()
            else:
                mine[j] = part
        remote(away.at[j], sib.at[j], sib_send.at[j], sib_recv.at[j], sibling).wait()

        @pl.when(k < nc - 1)
        def _():
            @pl.loop(0, count, step=step)
            def _(r):
                at = pl.ds(pl.multiple_of(r, step), step)
                mine[j, at, :] = (
                    mine[j, at, :].astype(F32) + sib[j, at, :].astype(F32)
                ).astype(BF)

            remote(
                mine.at[j], far.at[chip], send.at[j], recv.at[chip], (2 * j + core, z)
            ).start()

        @pl.when((k > 0) & (k < n_z))
        def _():
            sz = chain_take(n_z, k, *chain)
            rows_out(
                n_e,
                cap,
                k - 1,
                sz,
                zbuf.at[sz],
                pick_ref,
                rows,
                dy_ref,
                r_own,
                r_send,
                r_recv,
            )

    @pl.loop(0, count, step=step)
    def _(r):
        at = pl.ds(pl.multiple_of(r, step), step)
        total_ref[at, :] = mine[chip, at, :].astype(F32) + sib[chip, at, :].astype(F32)

    for k in range(nc - 1, 0, -1):
        j = partner_chip(chip, k)
        remote(
            mine.at[j], far.at[j], send.at[j], recv.at[j], (2 * j + core, z)
        ).wait()

        @pl.loop(0, count, step=step)
        def _(r, j=j):
            at = pl.ds(pl.multiple_of(r, step), step)
            total_ref[at, :] += far[j, at, :].astype(F32)

    for slot, b in enumerate(blocks(nc - 1)[1]):
        for copy in stores(b, slot):
            copy.wait()
    for k in range(1, n_z):
        rows_out_wait(
            n_e, cap, k - 1, ranked(z, k, n_z), rows, dy_ref, r_own, r_send, r_recv
        )
    chain_end(n_z, ct_ref, *chain)


def front(n_e, n_z, cap, heads, xs, ct, picks, turn_table, seg, w, wo, g1, gh):
    _, count, width = xs.shape
    nc = n_e // 2
    outs = ((width, BF), ((heads + 1) * HEAD, F32), (HEAD, BF), (heads * HEAD, BF))
    bufs = [pltpu.VMEM((2, count, width), BF)]
    bufs += [pltpu.VMEM((2, count, c), t) for c, t in outs]
    bufs += [pltpu.VMEM((nc, count, width), BF)] * 4
    bufs += [
        pltpu.VMEM((n_z, count, width), BF),
        pltpu.VMEM((n_z - 1, n_e * cap, width), BF),
    ]
    return pl.pallas_call(
        partial(front_kernel, n_e, n_z, cap, heads),
        out_shape=tuple(jax.ShapeDtypeStruct((n_e, count, c), t) for c, t in outs)
        + (
            jax.ShapeDtypeStruct((count, width), F32),
            jax.ShapeDtypeStruct((n_z, n_e, cap, width), BF),
        ),
        in_specs=[ANY] + [VM] * 8,
        out_specs=(ANY,) * 4 + (VM, ANY),
        scratch_shapes=bufs
        + [
            DMA((2,)),
            DMA((4, 2)),
            DMA((nc,)),
            DMA((nc,)),
            DMA((nc,)),
            DMA((nc,)),
            DMA((n_z + 1,)),
            DMA((n_z,)),
            DMA((n_z, n_e)),
            DMA((n_z, n_e)),
            DMA((n_z,)),
        ],
        compiler_params=pltpu.CompilerParams(
            collective_id=12, has_side_effects=True, vmem_limit_bytes=BIG
        ),
        name="front",
    )(xs, ct, picks, turn_table, seg, w, wo, g1, gh)


def norm_back(u, gain, dv):
    r = lax.rsqrt(jnp.mean(u * u, axis=-1, keepdims=True) + EPSILON)
    nu = u * r
    dgain = jnp.sum(dv * nu, axis=0, keepdims=True)
    scaled = dv * gain
    du = r * (scaled - nu * jnp.mean(scaled * nu, axis=-1, keepdims=True))
    return du, dgain


def attend_back_block(
    heads,
    da,
    n1,
    raw_ref,
    value,
    cos,
    sin,
    allowed,
    w_ref,
    wo_ref,
    gh_ref,
    dmix,
    dcat,
    g1_ref,
    ghg_ref,
):
    dmix[...] = dot_last(da, wo_ref[...]).astype(BF)
    gq, gk = gh_ref[0:1, :], gh_ref[1:2, :]
    qk = (heads + 1) * HEAD
    key_raw = raw_ref[:, heads * HEAD : qk]
    key = turn(head_norm(key_raw, gk), cos, sin).astype(BF)
    count = key.shape[0]
    dkey = jnp.zeros((count, HEAD), F32)
    dvalue = jnp.zeros((count, HEAD), F32)
    dgq = jnp.zeros((1, HEAD), F32)
    scale = HEAD**-0.5
    for h in range(heads):
        at = slice(h * HEAD, (h + 1) * HEAD)
        query_raw = raw_ref[:, at]
        query = turn(head_norm(query_raw, gq), cos, sin).astype(BF)
        weight = probabilities(query, key, allowed)
        dm = dmix[:, at]
        dweight = dot_last(dm, value)
        delta = jnp.sum(weight * dweight, axis=-1, keepdims=True)
        dscore = (weight * (dweight - delta)).astype(BF)
        dquery = dot(dscore, key) * scale
        dkey += dot_first(dscore, query) * scale
        dvalue += dot_first(weight.astype(BF), dm)
        du, dg = norm_back(query_raw, gq, turn_back(dquery, cos, sin))
        dcat[:, at] = du.astype(BF)
        dgq += dg
    du, dgk = norm_back(key_raw, gk, turn_back(dkey, cos, sin))
    dcat[:, heads * HEAD : qk] = du.astype(BF)
    dcat[:, qk:] = dvalue.astype(BF)
    ghg_ref[0:1, :] += dgq
    ghg_ref[1:2, :] += dgk
    dn = dot_last(dcat[...], w_ref[...])
    g1_ref[...] += jnp.sum(dn * n1.astype(F32), axis=0, keepdims=True)
    return dn.astype(BF)


def attend_back_kernel(
    heads,
    steps,
    da_ref,
    n1_ref,
    raw_ref,
    v_ref,
    mix_ref,
    turn_ref,
    seg_ref,
    w_ref,
    wo_ref,
    gh_ref,
    dn_ref,
    gw_ref,
    go_ref,
    g1_ref,
    ghg_ref,
    acc_w,
    acc_o,
    dcat,
    dmix,
):
    step = pl.program_id(0)

    @pl.when(step == 0)
    def _():
        acc_w[...] = jnp.zeros_like(acc_w)
        acc_o[...] = jnp.zeros_like(acc_o)
        g1_ref[...] = jnp.zeros_like(g1_ref)
        ghg_ref[...] = jnp.zeros_like(ghg_ref)

    da, n1 = da_ref[0], n1_ref[0]
    dn_ref[0] = attend_back_block(
        heads,
        da,
        n1,
        raw_ref.at[0],
        v_ref[0],
        *turns(turn_ref[0]),
        may_see(seg_ref[0]),
        w_ref,
        wo_ref,
        gh_ref,
        dmix,
        dcat,
        g1_ref,
        ghg_ref,
    )
    acc_w[...] += dot_first(n1, dcat[...])
    acc_o[...] += dot_first(mix_ref[0], da)

    @pl.when(step == steps - 1)
    def _():
        gw_ref[...] = acc_w[...].astype(BF)
        go_ref[...] = acc_o[...].astype(BF)


def attend_back(n_e, heads, da, n1, raw, v, mix, turn_table, seg, w, wo, gh):
    _, count, width = da.shape

    def block(*shape):
        return pl.BlockSpec((1,) + shape, lambda b: (b, 0, 0))

    def whole(*shape):
        return pl.BlockSpec(shape, lambda b: (0, 0))

    return pl.pallas_call(
        partial(attend_back_kernel, heads, n_e),
        grid=(n_e,),
        out_shape=(
            jax.ShapeDtypeStruct((n_e, count, width), BF),
            jax.ShapeDtypeStruct(w.shape, BF),
            jax.ShapeDtypeStruct(wo.shape, BF),
            jax.ShapeDtypeStruct((1, width), F32),
            jax.ShapeDtypeStruct((8, HEAD), F32),
        ),
        in_specs=[
            block(count, width),
            block(count, width),
            block(*raw.shape[1:]),
            block(count, HEAD),
            block(*mix.shape[1:]),
            block(count, HEAD),
            block(1, count),
            whole(*w.shape),
            whole(*wo.shape),
            whole(*gh.shape),
        ],
        out_specs=(
            block(count, width),
            whole(*w.shape),
            whole(*wo.shape),
            whole(1, width),
            whole(8, HEAD),
        ),
        scratch_shapes=[
            pltpu.VMEM(w.shape, F32),
            pltpu.VMEM(wo.shape, F32),
            pltpu.VMEM((count, (heads + 2) * HEAD), BF),
            pltpu.VMEM((count, heads * HEAD), BF),
        ],
        compiler_params=pltpu.CompilerParams(vmem_limit_bytes=BIG),
        name="attend_back",
    )(da, n1, raw, v, mix, turn_table, seg, w, wo, gh)


def back_kernel(
    n_e,
    n_z,
    cap,
    heads,
    da_ref,
    r_ref,
    rfar_ref,
    gr_ref,
    n1_ref,
    raw_ref,
    v_ref,
    mix_ref,
    unpick_ref,
    g2_ref,
    turn_ref,
    seg_ref,
    w_ref,
    wo_ref,
    g1_ref,
    gh_ref,
    total_ref,
    part_ref,
    gws_ref,
    goo_ref,
    gor_ref,
    gol_ref,
    grs_ref,
    gvs_ref,
    ret_ref,
    gwr_ref,
    gwl_ref,
    rsum,
    gplane,
    das,
    n1s,
    raws,
    vs,
    mixs,
    dcats,
    dmix,
    gsum,
    ghsum,
    gvec,
    gtotal,
    away,
    mine,
    sib,
    far,
    rbuf,
    gob,
    own,
    in_sem,
    raw_sem,
    d_send,
    d_recv,
    ds_send,
    ds_recv,
    a_send,
    a_recv,
    b_send,
    b_recv,
    b_own,
    p_send,
    p_recv,
    o_send,
    or_recv,
    ol_recv,
    w_send,
    wr_recv,
    wl_recv,
    s_send,
    s_recv,
    t_sem,
    v_send,
    v_recv,
    vz_send,
    vz_recv,
    sib_send,
    sib_recv,
    send,
    recv,
):
    e, z = place()
    n, me = n_e * n_z, e * n_z + z
    nc, chip, core = n_e // 2, e // 2, lax.rem(e, 2)
    sibling = (2 * chip + 1 - core, z)
    count, width = total_ref.shape
    shard = width // n
    head_rows = mixs.shape[-1] // n_z
    step = 32
    greet_all(n_e, n_z)

    def other_of(k):
        other = lax.rem(me + k, n)
        return other, (other // n_z, lax.rem(other, n_z))

    def far_chip(k):
        return (2 * partner_chip(chip, k) + core, z)

    def give_da(k):
        return remote(
            da_ref, das.at[e], d_send.at[k], d_recv.at[chip], far_chip(k)
        )

    remote(da_ref, das.at[e], ds_send.at[0], ds_recv.at[chip], sibling).start()
    for k in range(1, nc - 1):
        give_da(k).start()
    own_da = pltpu.make_async_copy(da_ref, das.at[e], own.at[0])
    own_da.start()

    @pl.loop(1, n)
    def _(k):
        other, where = other_of(k)
        remote(
            gr_ref.at[other], grs_ref.at[me], a_send.at[k], a_recv.at[me], where
        ).start()

    own_gr = pltpu.make_async_copy(gr_ref.at[me], grs_ref.at[me], own.at[1])
    own_gr.start()
    for i, (src, dst) in enumerate(((n1_ref, n1s), (v_ref, vs), (mix_ref, mixs))):
        pltpu.make_async_copy(src, dst, in_sem.at[i]).start()

    def load_raw(b, slot):
        return pltpu.make_async_copy(raw_ref.at[b], raws.at[slot], raw_sem.at[slot])

    def blocks(k):
        j = partner_chip(chip, k)
        return j, (2 * j + core, 2 * j + 1 - core)

    def source(k):
        return jnp.where(k == 0, z, ranked(z, k, n_z))

    def give_rows(k):
        sz = source(k)
        for i in range(1, n_e):
            oe = lax.rem(e + i, n_e)
            remote(
                r_ref.at[sz, oe],
                ret_ref.at[sz, e],
                b_send.at[k, i],
                b_recv.at[sz, e],
                (oe, z),
            ).start()
        pltpu.make_async_copy(r_ref.at[sz, e], ret_ref.at[sz, e], b_own.at[k]).start()

    for slot in range(2):
        load_raw(blocks(0)[1][slot], slot).start()
    gsum[...] = jnp.zeros_like(gsum)
    ghsum[...] = jnp.zeros_like(ghsum)
    for i, (src, dst) in enumerate(((n1_ref, n1s), (v_ref, vs), (mix_ref, mixs))):
        pltpu.make_async_copy(src, dst, in_sem.at[i]).wait()

    tokens = n_e * count

    def out_weights():
        da_all = das[...].reshape(tokens, width)
        for oz in range(n_z):
            at = slice(oz * head_rows, (oz + 1) * head_rows)
            gob[oz] = dot_first(mixs[:, :, at].reshape(tokens, head_rows), da_all).astype(BF)
        pass_all(out_pass, 0)

    def pass_sum(d, step, stage, block, inbox, recv, send, add):
        distance = z if step > 0 else n_z - 1 - z
        going = (d > z) if step > 0 else (d < z)

        @pl.when(going & (distance == stage))
        def _():
            if stage:
                remote(block, inbox.at[d], send.at[d], recv.at[d], (e, z - step)).wait_recv()
                add(d, inbox)
            remote(block, inbox.at[d], send.at[d], recv.at[d], (e, z + step)).start()

    def pass_all(one_pass, stage):
        for d in range(n_z - 1):
            one_pass(n_z - 1 - d, 1, stage)
            one_pass(d, -1, stage)

    def out_add(d, inbox):
        fetch = pltpu.make_async_copy(inbox.at[d], away.at[0:head_rows], t_sem.at[0])
        fetch.start()
        fetch.wait()

        @pl.loop(0, head_rows, step=step)
        def _(r):
            at = pl.ds(pl.multiple_of(r, step), step)
            gob[d, at, :] = (gob[d, at, :].astype(F32) + away[at, :].astype(F32)).astype(BF)

    def out_pass(d, step, stage):
        inbox, recv = (gor_ref, or_recv) if step > 0 else (gol_ref, ol_recv)
        pass_sum(d, step, stage, gob.at[d], inbox, recv, o_send, out_add)

    parts = dcats.shape[-1] // (n_z * shard)

    def shard_at(d):
        return pl.ds(pl.multiple_of(d * shard, shard), shard)

    def weight_add(d, inbox):
        for p in range(parts):
            there = away.at[p * shard : (p + 1) * shard]
            pltpu.make_async_copy(inbox.at[d, p], there, t_sem.at[p]).start()
        for p in range(parts):
            there = away.at[p * shard : (p + 1) * shard]
            pltpu.make_async_copy(inbox.at[d, p], there, t_sem.at[p]).wait()

            @pl.loop(0, shard, step=step)
            def _(r, p=p):
                at = pl.ds(pl.multiple_of(d * shard + r, step), step)
                came = away[pl.ds(pl.multiple_of(p * shard + r, step), step), :]
                n1s[p, at, :] = (n1s[p, at, :].astype(F32) + came.astype(F32)).astype(BF)

    def weight_pass(d, step, stage):
        inbox, recv = (gwr_ref, wr_recv) if step > 0 else (gwl_ref, wl_recv)
        block = n1s.at[0:parts, shard_at(d), :]
        pass_sum(d, step, stage, block, inbox, recv, w_send, weight_add)

    def sum_rows(src, dst, k):
        sz = source(k)
        unpick = unpick_ref[sz]
        cuts = pieces(width, 256)

        def fetch(p):
            start, size = cuts[p]
            return pltpu.make_async_copy(
                src.at[:, :, start : start + size], rbuf.at[p % 2], in_sem.at[p % 2]
            )

        fetch(0).start()
        for p, (start, size) in enumerate(cuts):
            if p + 1 < len(cuts):
                fetch(p + 1).start()
            fetch(p).wait()
            block = rbuf[p % 2].reshape(n_e * cap, size)
            dst[:, start : start + size] = dot(unpick, block).astype(BF)

    def sum_of(k):
        return rsum if k == n_z - 1 else das.at[k]

    def send_sum(k):
        sz = source(k)
        return remote(sum_of(k), part_ref.at[z], p_send.at[k], p_recv.at[z], (e, sz))

    def take_rows(k):
        sz = source(k)
        for i in range(1, n_e):
            oe = lax.rem(e + i, n_e)
            remote(
                r_ref.at[sz, oe],
                ret_ref.at[sz, oe],
                b_send.at[k, i],
                b_recv.at[sz, oe],
                (oe, z),
            ).wait()
        pltpu.make_async_copy(r_ref.at[sz, e], ret_ref.at[sz, e], b_own.at[k]).wait()
        sum_rows(ret_ref.at[sz], sum_of(k), k)

    sum_rows(rfar_ref, rsum, n_z - 1)
    send_sum(n_z - 1).start()

    @pl.loop(0, nc)
    def _(k):
        j, pair = blocks(k)

        @pl.when(k == 0)
        def _():
            pltpu.make_async_copy(da_ref, das.at[e], own.at[0]).wait()

        @pl.when(k > 0)
        def _():
            block = das.at[2 * j + core]
            remote(da_ref, block, d_send.at[k], d_recv.at[j], far_chip(k)).wait_recv()
            remote(block, block, ds_send.at[k], ds_recv.at[j], sibling).start()

        def sibling_da():
            remote(
                da_ref, das.at[pair[1]], ds_send.at[k], ds_recv.at[j], sibling
            ).wait_recv()

        @pl.when(k == nc - 1)
        def _():
            sibling_da()
            out_weights()

        for slot, b in enumerate(pair):
            if slot == 1:
                pl.when(k < nc - 1)(sibling_da)
            load_raw(b, slot).wait()
            part = attend_back_block(
                heads,
                das[b],
                n1s[b],
                raws.at[slot],
                vs[b],
                *turns(turn_ref[b]),
                may_see(seg_ref[b]),
                w_ref,
                wo_ref,
                gh_ref,
                dmix,
                dcats.at[b],
                gsum,
                ghsum,
            )

            @pl.when(k < nc - 1)
            def _(slot=slot):
                load_raw(blocks(k + 1)[1][slot], slot).start()

            if slot == 0:
                mine[j] = part
            else:
                away[...] = part
        to_sibling = remote(
            away, sib.at[lax.rem(k, 2)], sib_send, sib_recv.at[lax.rem(k, 2)], sibling
        )
        to_sibling.start()

        @pl.when(k == 0)
        def _():
            give_da(nc - 1).start()

        @pl.when((k > 0) & (k < n_z - 1))
        def _():
            give_rows(n_z - 1 - k)

        to_sibling.wait()

        @pl.when(k > 0)
        def _():
            @pl.loop(0, count, step=step)
            def _(r):
                at = pl.ds(pl.multiple_of(r, step), step)
                mine[j, at, :] = (
                    mine[j, at, :].astype(F32) + sib[lax.rem(k, 2), at, :].astype(F32)
                ).astype(BF)

            remote(
                mine.at[j], far.at[k - 1], send.at[k - 1], recv.at[k - 1], far_chip(k)
            ).start()

        @pl.when(k == 0)
        def _():
            @pl.loop(0, count, step=step)
            def _(r):
                at = pl.ds(pl.multiple_of(r, step), step)
                total_ref[at, :] = mine[j, at, :].astype(F32) + sib[0, at, :].astype(F32)

    remote(da_ref, das.at[e], ds_send.at[0], ds_recv.at[chip], sibling).wait_send()
    for k in range(1, nc):
        give_da(k).wait_send()
        block = das.at[2 * partner_chip(chip, k) + core]
        remote(block, block, ds_send.at[k], ds_recv.at[chip], sibling).wait_send()

    give_rows(0)
    pltpu.make_async_copy(gob.at[z], goo_ref, own.at[3]).start()
    pass_all(out_pass, 1)
    take_rows(n_z - 2)
    send_sum(n_z - 2).start()

    dcat = dcats[...].reshape(tokens, -1)

    @pl.loop(0, n_e)
    def _(t):
        at = pl.ds(pl.multiple_of(t * n_z * shard, n_z * shard), n_z * shard)
        rows = dot_first(n1s[:, :, at].reshape(tokens, n_z * shard), dcat).astype(BF)
        for p in range(parts):
            n1s[p, :, at] = rows[:, p * n_z * shard : (p + 1) * n_z * shard]

    pass_all(weight_pass, 0)

    lanes = 128
    g1 = gsum[...] / g1_ref[...]
    per = width // lanes
    for i in range(per):
        gvec[i : i + 1, :] = g1[:, i * lanes : (i + 1) * lanes]
        gvec[per + i : per + i + 1, :] = g2_ref[:, i * lanes : (i + 1) * lanes]
    gvec[2 * per : 2 * per + 8, :] = ghsum[...]

    for i in range(1, n_e):
        oe = lax.rem(e + i, n_e)
        remote(gvec, gplane.at[e], v_send.at[i], v_recv.at[e], (oe, z)).start()
    gplane[e] = gvec[...]
    for k in range(1, nc):
        j = partner_chip(chip, k)
        remote(
            mine.at[j], far.at[k - 1], send.at[k - 1], recv.at[k - 1], far_chip(k)
        ).wait()

        @pl.loop(0, count, step=step)
        def _(r, k=k):
            at = pl.ds(pl.multiple_of(r, step), step)
            total_ref[at, :] += far[k - 1, at, :].astype(F32)

    pass_all(out_pass, 2)
    for k in range(n_z - 3, 0, -1):
        take_rows(k)
        send_sum(k).start()
    pass_all(weight_pass, 1)
    take_rows(0)
    pltpu.make_async_copy(das.at[0], part_ref.at[z], own.at[6]).start()
    pass_all(weight_pass, 2)

    for came, inbox, recv_w, there in (
        (z > 0, gwr_ref, wr_recv, z - 1),
        (z < n_z - 1, gwl_ref, wl_recv, z + 1),
    ):

        @pl.when(came)
        def _(inbox=inbox, recv_w=recv_w, there=there):
            block = n1s.at[0:parts, shard_at(z), :]
            remote(block, inbox.at[z], w_send.at[z], recv_w.at[z], (e, there)).wait_recv()
            weight_add(z, inbox)

    def weight_block(t):
        at = pl.ds(pl.multiple_of(t * n_z * shard, n_z * shard), n_z * shard)
        return n1s.at[0:parts, shard_at(z), at]

    for i in range(1, n_e):
        oe = lax.rem(e + i, n_e)
        remote(weight_block(oe), gws_ref.at[e], s_send.at[i], s_recv.at[e], (oe, z)).start()
    pltpu.make_async_copy(weight_block(e), gws_ref.at[e], own.at[2]).start()
    for i in range(1, n_e):
        oe = lax.rem(e + i, n_e)
        remote(gvec, gplane.at[oe], v_send.at[i], v_recv.at[oe], (oe, z)).wait()
    gtotal[...] = jnp.sum(gplane[...], axis=0)
    for k in range(1, n_z):
        oz = near(z, k, n_z)
        remote(gtotal, gvs_ref.at[z], vz_send.at[k], vz_recv.at[z], (e, oz)).start()
    own_gv = pltpu.make_async_copy(gtotal, gvs_ref.at[z], own.at[4])
    own_gv.start()

    @pl.loop(1, n)
    def _(k):
        other, where = other_of(k)
        remote(
            gr_ref.at[other],
            grs_ref.at[other],
            a_send.at[k],
            a_recv.at[other],
            where,
        ).wait()

    for i in range(1, n_e):
        oe = lax.rem(e + i, n_e)
        remote(weight_block(oe), gws_ref.at[oe], s_send.at[i], s_recv.at[oe], (oe, z)).wait()
    for d in range(n_z):

        @pl.when(d != z)
        def _(d=d):
            remote(gob.at[d], gor_ref.at[d], o_send.at[d], or_recv.at[d], (e, d)).wait_send()
            block = n1s.at[0:parts, shard_at(d), :]
            remote(block, gwr_ref.at[d], w_send.at[d], wr_recv.at[d], (e, d)).wait_send()

    for came, inbox, recv_o, there in (
        (z > 0, gor_ref, or_recv, z - 1),
        (z < n_z - 1, gol_ref, ol_recv, z + 1),
    ):

        @pl.when(came)
        def _(inbox=inbox, recv_o=recv_o, there=there):
            remote(
                gob.at[z], inbox.at[z], o_send.at[z], recv_o.at[z], (e, there)
            ).wait_recv()

    for k in range(1, n_z):
        oz = near(z, k, n_z)
        remote(
            gtotal, gvs_ref.at[oz], vz_send.at[k], vz_recv.at[oz], (e, oz)
        ).wait()
        sz = ranked(z, k, n_z)
        remote(
            sum_of(k), part_ref.at[sz], p_send.at[k], p_recv.at[sz], (e, sz)
        ).wait()
    own_gr.wait()
    pltpu.make_async_copy(weight_block(e), gws_ref.at[e], own.at[2]).wait()
    pltpu.make_async_copy(gob.at[z], goo_ref, own.at[3]).wait()
    own_gv.wait()
    pltpu.make_async_copy(das.at[0], part_ref.at[z], own.at[6]).wait()


def back(
    n_e, n_z, cap, heads, da, r_rows, r_far, gr, n1, raw, v, mix, unpicks, g2, turn_table, seg, w, wo, g1, gh
):
    n, nc = n_e * n_z, n_e // 2
    count, width = da.shape
    shard = width // n
    columns = w.shape[1]
    parts = columns // (n_z * shard)
    out_block = (wo.shape[0] // n_z, width)
    vec_rows = 2 * width // 128 + 8
    block = (count, width)

    def sems(*shape):
        return DMA(shape)

    return pl.pallas_call(
        partial(back_kernel, n_e, n_z, cap, heads),
        out_shape=(
            jax.ShapeDtypeStruct(block, F32),
            jax.ShapeDtypeStruct((n_z,) + block, BF),
            jax.ShapeDtypeStruct((n_e, parts, shard, n_z * shard), BF),
            jax.ShapeDtypeStruct(out_block, BF),
            jax.ShapeDtypeStruct((n_z,) + out_block, BF),
            jax.ShapeDtypeStruct((n_z,) + out_block, BF),
            jax.ShapeDtypeStruct(gr.shape, F32),
            jax.ShapeDtypeStruct((n_z, vec_rows, 128), F32),
            jax.ShapeDtypeStruct(r_rows.shape, BF),
            jax.ShapeDtypeStruct((n_z, parts, shard, width), BF),
            jax.ShapeDtypeStruct((n_z, parts, shard, width), BF),
        ),
        in_specs=[ANY] * 8 + [VM] * 8,
        out_specs=(VM,) + (ANY,) * 10,
        scratch_shapes=[
            pltpu.VMEM(block, BF),
            pltpu.VMEM((n_e, vec_rows, 128), F32),
            pltpu.VMEM((n_e,) + block, BF),
            pltpu.VMEM(n1.shape, BF),
            pltpu.VMEM((2,) + raw.shape[1:], F32),
            pltpu.VMEM(v.shape, BF),
            pltpu.VMEM(mix.shape, BF),
            pltpu.VMEM((n_e, count, columns), BF),
            pltpu.VMEM((count, heads * HEAD), BF),
            pltpu.VMEM((1, width), F32),
            pltpu.VMEM((8, HEAD), F32),
            pltpu.VMEM((vec_rows, 128), F32),
            pltpu.VMEM((vec_rows, 128), F32),
            pltpu.VMEM(block, BF),
            pltpu.VMEM((nc,) + block, BF),
            pltpu.VMEM((2,) + block, BF),
            pltpu.VMEM((nc - 1,) + block, BF),
            pltpu.VMEM((2, n_e, cap, 256), BF),
            pltpu.VMEM((n_z, wo.shape[0] // n_z, width), BF),
            sems(7),
            sems(3),
            sems(2),
            sems(nc),
            sems(nc),
            sems(nc),
            sems(nc),
            sems(n),
            sems(n),
            sems(n_z, n_e),
            sems(n_z, n_e),
            sems(n_z),
            sems(n_z),
            sems(n_z),
            sems(n_z),
            sems(n_z),
            sems(n_z),
            sems(n_z),
            sems(n_z),
            sems(n_z),
            sems(n_e),
            sems(n_e),
            sems(parts),
            sems(n_e),
            sems(n_e),
            sems(n_z),
            sems(n_z),
            DMA,
            sems(2),
            sems(nc),
            sems(nc),
        ],
        compiler_params=pltpu.CompilerParams(
            collective_id=14, has_side_effects=True, vmem_limit_bytes=63 * 1024 * 1024
        ),
        name="back",
    )(da, r_rows, r_far, gr, n1, raw, v, mix, unpicks, g2, turn_table, seg, w, wo, g1, gh)


def expert_kernel(
    n_z,
    experts,
    width,
    x_ref,
    dy_ref,
    wg_ref,
    wu_ref,
    wd_ref,
    r_ref,
    dx_ref,
    gg_ref,
    gu_ref,
    gd_ref,
):
    step = pl.program_id(0)

    @pl.when(step == 0)
    def _():
        gg_ref[...] = jnp.zeros_like(gg_ref)
        gu_ref[...] = jnp.zeros_like(gu_ref)
        gd_ref[...] = jnp.zeros_like(gd_ref)

    e, z = place()
    me = e * n_z + z
    x = x_ref[:, :width]
    extra = x_ref[:, width:].astype(F32)
    lane = lax.broadcasted_iota(jnp.int32, extra.shape, 1)
    gate = jnp.sum(
        jnp.where((lane == me) | (lane == experts + me), extra, 0.0), axis=1, keepdims=True
    )
    gate_part = dot(x, wg_ref[...])
    up_part = dot(x, wu_ref[...])
    sig = 1.0 / (1.0 + jnp.exp(-gate_part))
    act = gate_part * sig
    inner = (act * up_part).astype(BF)
    r_ref[...] = (dot(inner, wd_ref[...]) * gate).astype(BF)
    dy = dy_ref[...]
    dinner = dot_last(dy, wd_ref[...])
    inner_f = inner.astype(F32)
    dgate = jnp.sum(dinner * inner_f, axis=1, keepdims=True)
    gd_ref[...] += dot_first((inner_f * gate).astype(BF), dy)
    dinner = dinner * gate
    dgp = (dinner * up_part * sig * (1.0 + gate_part * (1.0 - sig))).astype(BF)
    dup = (dinner * act).astype(BF)
    dx_ref[:, :width] = (dot_last(dgp, wg_ref[...]) + dot_last(dup, wu_ref[...])).astype(BF)
    high = dgate.astype(BF).astype(F32)
    dx_ref[:, width:] = jnp.where(
        lane == me, high, jnp.where(lane == experts + me, dgate - high, 0.0)
    ).astype(BF)
    gg_ref[...] += dot_first(x, dgp)
    gu_ref[...] += dot_first(x, dup)


def expert_run(n_z, experts, x, dy, wg, wu, wd):
    rows, columns = x.shape
    width, hidden = wg.shape
    tile = 512

    def block(c):
        return pl.BlockSpec((tile, c), lambda b: (b, 0))

    def whole(shape):
        return pl.BlockSpec(shape, lambda b: (0, 0), pipeline_mode=pl.Buffered(1))

    return pl.pallas_call(
        partial(expert_kernel, n_z, experts, width),
        grid=(rows // tile,),
        out_shape=(
            jax.ShapeDtypeStruct((rows, width), BF),
            jax.ShapeDtypeStruct((rows, columns), BF),
            jax.ShapeDtypeStruct((width, hidden), F32),
            jax.ShapeDtypeStruct((width, hidden), F32),
            jax.ShapeDtypeStruct((hidden, width), F32),
        ),
        in_specs=[
            block(columns),
            block(width),
            whole(wg.shape),
            whole(wu.shape),
            whole(wd.shape),
        ],
        out_specs=(
            block(width),
            block(columns),
            whole(wg.shape),
            whole(wu.shape),
            whole(wd.shape),
        ),
        compiler_params=pltpu.CompilerParams(vmem_limit_bytes=BIG),
        name="experts",
    )(x, dy, wg, wu, wd)


def expert_tile(width, experts, me, x_ext, dy, wg_ref, wu_ref, wd_ref):
    x = x_ext[:, :width]
    extra = x_ext[:, width:].astype(F32)
    lane = lax.broadcasted_iota(jnp.int32, extra.shape, 1)
    gate = jnp.sum(
        jnp.where((lane == me) | (lane == experts + me), extra, 0.0), axis=1, keepdims=True
    )
    gate_part = dot(x, wg_ref[...])
    up_part = dot(x, wu_ref[...])
    sig = 1.0 / (1.0 + jnp.exp(-gate_part))
    act = gate_part * sig
    inner = (act * up_part).astype(BF)
    result = (dot(inner, wd_ref[...]) * gate).astype(BF)
    dinner = dot_last(dy, wd_ref[...])
    inner_f = inner.astype(F32)
    dgate = jnp.sum(dinner * inner_f, axis=1, keepdims=True)
    gated = (inner_f * gate).astype(BF)
    dinner = dinner * gate
    dgp = (dinner * up_part * sig * (1.0 + gate_part * (1.0 - sig))).astype(BF)
    dup = (dinner * act).astype(BF)
    dx = (dot_last(dgp, wg_ref[...]) + dot_last(dup, wu_ref[...])).astype(BF)
    high = dgate.astype(BF).astype(F32)
    back = jnp.where(
        lane == me, high, jnp.where(lane == experts + me, dgate - high, 0.0)
    ).astype(BF)
    return result, dx, back, gated, dgp, dup


def moe_kernel(
    n_e,
    n_z,
    cap,
    tok_ref,
    pick_ref,
    unpick_ref,
    near_ref,
    far_ref,
    wg_ref,
    wu_ref,
    wd_ref,
    xs_ref,
    r_ref,
    dx_ref,
    ret_ref,
    part_ref,
    gi_ref,
    dg_ref,
    du_ref,
    gg_ref,
    gu_ref,
    gd_ref,
    rret_ref,
    zbuf,
    z_send,
    z_recv,
    r_send,
    r_recv,
    r_own,
    in_sem,
    out_sem,
    b_send,
    b_recv,
    b_own,
    p_send,
    p_recv,
    p_own,
    e_send,
    e_recv,
    g_sem,
    t_sem,
    w_sem,
):
    e, z = place()
    me = e * n_z + z
    width = far_ref.shape[-1]
    hidden = wd_ref.shape[0]
    experts = n_e * n_z
    columns = tok_ref.shape[-1]
    last = n_z - 1
    inner = (z > 0) & (z < last)
    greet(n_e, n_z, True)
    chain = (lambda s: zbuf.at[s], z_send, z_recv)
    chain_start(n_z, tok_ref, *chain)

    def source(k):
        return jnp.where(k == 0, z, ranked(z, k, n_z))

    def give_one(k, i):
        sz, oe = source(k), lax.rem(e + i, n_e)
        return remote(
            dx_ref.at[sz, oe],
            ret_ref.at[sz, e],
            b_send.at[k, i],
            b_recv.at[sz, e],
            (oe, z),
        )

    def give_own(k):
        sz = source(k)
        return pltpu.make_async_copy(dx_ref.at[sz, e], ret_ref.at[sz, e], b_own.at[k])

    def give(k):
        for i in range(1, n_e):
            give_one(k, i).start()
        give_own(k).start()

    def store(k, tiles, i):
        src, dst = tiles[i]
        return pltpu.make_async_copy(src, dst.at[source(k)], out_sem.at[i])

    def first_phase(rows, xt, yt, rt, dxt, git, dgt, dut):
        out_args = (xs_ref, r_own, r_send, r_recv)
        rows_out(n_e, cap, 0, z, tok_ref, pick_ref, rows, *out_args)
        tiles = ((dxt, dx_ref), (rt, r_ref), (git, gi_ref), (dgt, dg_ref), (dut, du_ref))

        def load_y(src):
            return pltpu.make_async_copy(src, yt, in_sem.at[1])

        @pl.loop(0, n_z)
        def _(k):
            sz = source(k)

            @pl.when(k == 0)
            def _():
                load_y(near_ref).start()

            @pl.when(k > 0)
            def _():
                load_y(far_ref.at[sz]).start()

            @pl.when(jnp.where(inner, k == 0, k < last))
            def _():
                chain_take(n_z, k + 1, *chain)

            @pl.when(inner & (k + 2 < n_z))
            def _():
                chain_take(n_z, k + 2, *chain)

            @pl.when(k < last)
            def _():
                nz = source(k + 1)
                rows_out(n_e, cap, k + 1, nz, zbuf.at[nz], pick_ref, rows, *out_args)

            rows_out_wait(n_e, cap, k, sz, rows, *out_args)
            fetch = pltpu.make_async_copy(xs_ref.at[sz], xt, in_sem.at[0])
            fetch.start()
            fetch.wait()
            load_y(far_ref.at[sz]).wait()

            @pl.when((k > 0) & (k < last))
            def _():
                store(k, tiles, 0).wait()

            @pl.when(k > 0)
            def _():
                for i in range(1, 5):
                    store(k, tiles, i).wait()

            result, dx, back, gated, dgp, dup = expert_tile(
                width,
                experts,
                me,
                xt[...].reshape(n_e * cap, -1),
                yt[...].reshape(n_e * cap, -1),
                wg_ref,
                wu_ref,
                wd_ref,
            )
            rt[...] = result.reshape(n_e, cap, -1)
            dxt[:, :, :width] = dx.reshape(n_e, cap, -1)
            dxt[:, :, width:] = back.reshape(n_e, cap, -1)
            git[...] = gated.reshape(n_e, cap, -1)
            dgt[...] = dgp.reshape(n_e, cap, -1)
            dut[...] = dup.reshape(n_e, cap, -1)
            for i in range(5):
                store(k, tiles, i).start()

            @pl.when(k >= last - 1)
            def _():
                store(k, tiles, 0).wait()
                give(k)

        for i in range(1, 5):
            store(last, tiles, i).wait()

    def row_buffer(c):
        return pltpu.VMEM((n_e, cap, c), BF)

    pl.run_scoped(
        first_phase,
        pltpu.VMEM((n_z, n_e * cap, columns), BF),
        row_buffer(columns),
        row_buffer(width),
        row_buffer(width),
        row_buffer(columns),
        row_buffer(hidden),
        row_buffer(hidden),
        row_buffer(hidden),
    )
    chain_end(n_z, tok_ref, *chain)

    give(1)
    far_z = source(last)

    def give_result(i):
        oe = lax.rem(e + i, n_e)
        return remote(
            r_ref.at[far_z, oe], rret_ref.at[e], e_send.at[i], e_recv.at[e], (oe, z)
        )

    for i in range(1, n_e):
        give_result(i).start()
    own_result = pltpu.make_async_copy(r_ref.at[far_z, e], rret_ref.at[e], in_sem.at[0])
    own_result.start()
    give(0)
    size = 256
    count = width // size

    def second_phase(gis, dgs, dus, xc, yc, ggt, gut, gdt, rbuf):
        whole = ((gi_ref, gis), (dg_ref, dgs), (du_ref, dus))
        for i, (src, dst) in enumerate(whole):
            pltpu.make_async_copy(src, dst, g_sem.at[i]).start()

        def pairs(t):
            at = pl.ds(pl.multiple_of(t * size, size), size)
            slot = lax.rem(t, 2)
            copies = [
                pltpu.make_async_copy(xs_ref.at[:, :, :, at], xc.at[slot], t_sem.at[0, slot])
            ]
            for k in range(n_z):
                src = far_ref.at[source(k), :, :, at] if k else near_ref.at[:, :, at]
                copies.append(
                    pltpu.make_async_copy(
                        src, yc.at[slot, source(k)], t_sem.at[1 + k, slot]
                    )
                )
            return copies

        def results(t):
            at = pl.ds(pl.multiple_of(t * size, size), size)
            slot = lax.rem(t, 2)
            return [
                pltpu.make_async_copy(ggt.at[slot], gg_ref.at[at], w_sem.at[0, slot]),
                pltpu.make_async_copy(gut.at[slot], gu_ref.at[at], w_sem.at[1, slot]),
                pltpu.make_async_copy(gdt.at[slot], gd_ref.at[:, at], w_sem.at[2, slot]),
            ]

        def weight_tile(t):
            slot = lax.rem(t, 2)

            @pl.when(t + 1 < count)
            def _():
                for copy in pairs(t + 1):
                    copy.start()

            for copy in pairs(t):
                copy.wait()

            @pl.when(t >= 2)
            def _():
                for copy in results(t):
                    copy.wait()

            total = n_z * n_e * cap
            x = xc[slot].reshape(total, size)
            ggt[slot] = dot_first(x, dgs[...].reshape(total, hidden)).astype(BF)
            gut[slot] = dot_first(x, dus[...].reshape(total, hidden)).astype(BF)
            gdt[slot] = dot_first(
                gis[...].reshape(total, hidden), yc[slot].reshape(total, size)
            ).astype(BF)
            for copy in results(t):
                copy.start()

        def combine(k):
            sz = source(k)
            for i in range(1, n_e):
                oe = lax.rem(e + i, n_e)
                remote(
                    dx_ref.at[sz, oe],
                    ret_ref.at[sz, oe],
                    b_send.at[k, i],
                    b_recv.at[sz, oe],
                    (oe, z),
                ).wait()
            give_own(k).wait()
            unpick = unpick_ref[sz]
            cuts = pieces(columns)

            def fetch(p):
                start, wide = cuts[p]
                return pltpu.make_async_copy(
                    ret_ref.at[sz, :, :, start : start + wide],
                    rbuf.at[p % 2, :, :, 0:wide],
                    in_sem.at[1 + p % 2],
                )

            fetch(0).start()
            for p, (start, wide) in enumerate(cuts):
                if p + 1 < len(cuts):
                    fetch(p + 1).start()
                fetch(p).wait()
                block = rbuf[p % 2, :, :, 0:wide].reshape(n_e * cap, wide)
                zbuf[k, :, start : start + wide] = dot(unpick, block).astype(BF)

            @pl.when(k > 0)
            def _():
                remote(
                    zbuf.at[k], part_ref.at[z], p_send.at[k], p_recv.at[z], (e, sz)
                ).start()

            @pl.when(k == 0)
            def _():
                pltpu.make_async_copy(zbuf.at[k], part_ref.at[z], p_own).start()

        for copy in pairs(0):
            copy.start()
        for i, (src, dst) in enumerate(whole):
            pltpu.make_async_copy(src, dst, g_sem.at[i]).wait()
        share_of = count // n_z

        @pl.loop(0, n_z)
        def _(i):
            @pl.loop(0, share_of)
            def _(t):
                weight_tile(i * share_of + t)

            k = jnp.where(i == 0, last - 1, jnp.where(i == 1, last, last - i))
            combine(k)

        for t in (count - 2, count - 1):
            for copy in results(t):
                copy.wait()

    total_shape = (n_z, n_e, cap)
    pl.run_scoped(
        second_phase,
        pltpu.VMEM(total_shape + (hidden,), BF),
        pltpu.VMEM(total_shape + (hidden,), BF),
        pltpu.VMEM(total_shape + (hidden,), BF),
        pltpu.VMEM((2,) + total_shape + (size,), BF),
        pltpu.VMEM((2,) + total_shape + (size,), BF),
        pltpu.VMEM((2, size, hidden), BF),
        pltpu.VMEM((2, size, hidden), BF),
        pltpu.VMEM((2, hidden, size), BF),
        pltpu.VMEM((2, n_e, cap, pieces(columns)[0][1]), BF),
    )
    for i in range(1, n_e):
        oe = lax.rem(e + i, n_e)
        remote(
            r_ref.at[far_z, oe], rret_ref.at[oe], e_send.at[i], e_recv.at[oe], (oe, z)
        ).wait()
    own_result.wait()
    pltpu.make_async_copy(zbuf.at[0], part_ref.at[z], p_own).wait()
    for k in range(1, n_z):
        sz = ranked(z, k, n_z)
        remote(
            zbuf.at[k], part_ref.at[sz], p_send.at[k], p_recv.at[sz], (e, sz)
        ).wait()


def moe(n_e, n_z, cap, tok, picks, unpicks, dy_near, dy_far, wg, wu, wd):
    count, columns = tok.shape
    width, hidden = wg.shape

    def rows_of(c):
        return jax.ShapeDtypeStruct((n_z, n_e, cap, c), BF)

    return pl.pallas_call(
        partial(moe_kernel, n_e, n_z, cap),
        out_shape=(
            rows_of(columns),
            rows_of(width),
            rows_of(columns),
            rows_of(columns),
            jax.ShapeDtypeStruct((n_z, count, columns), BF),
            rows_of(hidden),
            rows_of(hidden),
            rows_of(hidden),
            jax.ShapeDtypeStruct((width, hidden), BF),
            jax.ShapeDtypeStruct((width, hidden), BF),
            jax.ShapeDtypeStruct((hidden, width), BF),
            jax.ShapeDtypeStruct((n_e, cap, width), BF),
        ),
        in_specs=[VM, VM, VM, ANY, ANY, VM, VM, VM],
        out_specs=(ANY,) * 12,
        scratch_shapes=[
            pltpu.VMEM((n_z, count, columns), BF),
            DMA((n_z + 1,)),
            DMA((n_z,)),
            DMA((n_z, n_e)),
            DMA((n_z, n_e)),
            DMA((n_z,)),
            DMA((3,)),
            DMA((5,)),
            DMA((n_z, n_e)),
            DMA((n_z, n_e)),
            DMA((n_z,)),
            DMA((n_z,)),
            DMA((n_z,)),
            DMA,
            DMA((n_e,)),
            DMA((n_e,)),
            DMA((3,)),
            DMA((1 + n_z, 2)),
            DMA((3, 2)),
        ],
        compiler_params=pltpu.CompilerParams(
            collective_id=13, has_side_effects=True, vmem_limit_bytes=63 * 1024 * 1024
        ),
        name="moe",
    )(tok, picks, unpicks, dy_near, dy_far, wg, wu, wd)


def layout(lengths, owners, device, row_count):
    seq_order = jnp.arange(lengths.shape[0], dtype=jnp.int32)
    owned = (owners == device).astype(jnp.int32)
    earlier = (seq_order[None, :] < seq_order[:, None]).astype(jnp.int32)
    starts = jnp.sum(earlier * (owned * lengths)[None, :], axis=1)
    row_index = jnp.arange(row_count, dtype=jnp.int32)
    inside = (
        owned[None, :]
        * (row_index[:, None] >= starts[None, :]).astype(jnp.int32)
        * (row_index[:, None] < (starts + lengths)[None, :]).astype(jnp.int32)
    )
    live_rows = jnp.sum(inside, axis=1)
    segment = jnp.sum(inside * (seq_order[None, :] + 1), axis=1) - 1
    token_position = jnp.sum(inside * (row_index[:, None] - starts[None, :]), axis=1)
    return (live_rows, segment, token_position)


def named_experts(routes, experts):
    return jnp.any(routes[..., None] == jnp.arange(experts, dtype=jnp.int32), axis=-2)


def slot_picks(n_e, n_z, z, cap, named, live):
    sources, count, experts = named.shape
    used = named & (live[:, :, None] > 0)
    order = jnp.arange(count)
    lower = (order[None, :] < order[:, None]).astype(BF)
    slots = jnp.einsum("ts,zse->zte", lower, used.astype(BF), preferred_element_type=F32)
    slots = jnp.where(used, slots, -1.0)
    column = jnp.arange(n_e * cap, dtype=jnp.int32)
    spread = (
        jnp.arange(experts, dtype=jnp.int32)[:, None] == (column // cap * n_z + z)[None, :]
    ).astype(BF)
    slots = slots.astype(BF)
    slot_ids = lax.rem(column, cap).astype(F32)
    picks = jnp.einsum("ec,ste->sct", spread, slots, preferred_element_type=F32)
    unpicks = jnp.einsum("ste,ec->stc", slots, spread, preferred_element_type=F32)
    return (
        (picks == slot_ids[None, :, None]).astype(BF),
        (unpicks == slot_ids).astype(BF),
    )


def split_float(values):
    high = values.astype(BF)
    return high, (values - high.astype(F32)).astype(BF)


def pad_lanes(values, lanes):
    return jnp.pad(values, ((0, 0), (0, lanes - values.shape[1])))


def local(
    n_e,
    n_z,
    tokens,
    cotangent,
    lengths,
    owners,
    routes,
    w_query,
    key_weight,
    value_weight,
    w_out,
    w_router,
    norm_gains,
    w_gate,
    w_up,
    w_down,
):
    n = n_e * n_z
    count, width = tokens.shape
    shard = w_query.shape[0]
    experts, top = w_router.shape[1], routes.shape[1]
    q_heads, kv_heads = w_query.shape[1] // HEAD, key_weight.shape[1] // HEAD
    heads = q_heads // n_e
    cap = count * top * 5 // (4 * experts)
    cap = -(-cap // 16) * 16
    e, z = place()

    wq_blocks = w_query.reshape(shard, n_e, heads * HEAD)
    sharing = n_e // kv_heads
    wk_blocks = jnp.repeat(key_weight.reshape(shard, kv_heads, HEAD), sharing, axis=1)
    wv_blocks = jnp.repeat(value_weight.reshape(shard, kv_heads, HEAD), sharing, axis=1)
    w_blocks = jnp.concatenate([wq_blocks, wk_blocks, wv_blocks], axis=2).transpose(1, 0, 2)
    router_rows = shard * experts // 128
    gain_rows = -(-norm_gains.shape[0] // 128)
    misc_rows = -(-(router_rows + gain_rows) // 16) * 16
    misc = jnp.concatenate(
        [
            w_router.reshape(-1),
            norm_gains,
            jnp.zeros((misc_rows - router_rows) * 128 - norm_gains.shape[0], BF),
        ]
    ).reshape(misc_rows, 128)
    routes_flat = routes.reshape(-1, 128)

    device = e * n_z + z
    plane_ids = jnp.arange(n_e, dtype=jnp.int32) * n_z + z
    column_ids = e * n_z + jnp.arange(n_z, dtype=jnp.int32)
    live_both, segment, position = jax.vmap(lambda d: layout(lengths, owners, d, count))(
        jnp.concatenate([plane_ids, column_ids])
    )
    live_all = live_both[n_e:]
    live_own = lax.dynamic_index_in_dim(live_all, z, keepdims=False)
    named_own = named_experts(routes, experts)
    small = n_e == 8 and n_z == 4
    if small:
        pick_own = slot_picks(n_e, n_z, z, cap, named_own[None], live_own[None])[0][0]
        xs, rts, w_all, wo_all, misc_all, dy_near = open_layer(
            n_e, n_z, cap, tokens, cotangent, routes_flat, w_blocks, w_out, misc, pick_own
        )
    else:
        xs, cts, rts, w_all, wo_all, misc_all = share(
            n_e, n_z, tokens, cotangent, routes_flat, w_blocks, w_out, misc
        )
    w_all = w_all.reshape(n * shard, -1)
    wo_all = wo_all.reshape(-1, width)
    router_w = misc_all[:, :router_rows].reshape(n * shard, experts)
    gains = (
        misc_all[:, router_rows:]
        .reshape(n, -1)[:, : norm_gains.shape[0]]
        .reshape(-1)
        .astype(F32)
    )
    gain_one = gains[None, :width]
    gain_two = gains[None, width : 2 * width]
    gain_heads = jnp.pad(gains[2 * width :].reshape(2, HEAD), ((0, 6), (0, 0)))

    half = HEAD // 2
    frequency = jnp.power(1000000.0, -2.0 * jnp.arange(half, dtype=F32) / HEAD)
    angles = position[:n_e].astype(F32)[:, :, None] * frequency
    turn_table = jnp.concatenate([jnp.cos(angles), jnp.sin(angles)], axis=-1)
    seg = segment[:n_e].astype(F32)[:, None, :]

    named_all = named_experts(rts.reshape(n_z, count, top), experts)
    picks, unpicks = slot_picks(n_e, n_z, z, cap, named_all, live_all)
    live = live_own.astype(F32)[:, None]
    named = named_own.astype(F32)

    shape = (turn_table, seg, w_all, wo_all, gain_one, gain_heads)
    if small:
        n1, raw, value, mix, attn_rows, dy_far = front(
            n_e, n_z, cap, heads, xs, cotangent, picks, *shape
        )
    else:
        dy_rows = send_rows(n_e, n_z, cap, cts, picks)
        n1, raw, value, mix, part = attend(n_e, heads, xs, *shape)
        attn_rows = plane_sum(n_e, n_z, part)

    inputs = tokens.astype(F32)
    hidden = inputs + live * attn_rows
    r_two = lax.rsqrt(jnp.mean(hidden * hidden, axis=-1, keepdims=True) + EPSILON)
    nu_two = hidden * r_two
    n2 = (nu_two * gain_two).astype(BF)
    logits = dot(n2, router_w)
    probs = jax.nn.softmax(logits, axis=-1)
    chosen = probs * named
    chosen_sum = jnp.sum(chosen, axis=1, keepdims=True)
    gates = chosen / chosen_sum
    lanes = -(-2 * experts // 128) * 128
    extra = pad_lanes(jnp.concatenate(split_float(gates), axis=1), lanes)
    tok = jnp.concatenate([n2, extra], axis=1)
    experts_w = (w_gate[0], w_up[0], w_down[0])
    if small:
        moved = moe(n_e, n_z, cap, tok, picks, unpicks, dy_near, dy_far, *experts_w)
        r_rows, dx_back = moved[1], moved[4]
        grad_gate, grad_up, grad_down = (a.astype(F32) for a in moved[8:11])
        r_far = moved[11]
    else:
        x_rows = dispatch(n_e, n_z, cap, tok, picks)
        r_rows, dx_rows, grad_gate, grad_up, grad_down = expert_run(
            n_z,
            experts,
            x_rows.reshape(-1, width + lanes),
            dy_rows.reshape(-1, width),
            *experts_w,
        )
        r_rows = r_rows.reshape(dy_rows.shape)
        dx_back = give_back(n_e, n_z, cap, dx_rows.reshape(x_rows.shape), unpicks, 6)

    dx_sum = jnp.sum(dx_back.astype(F32), axis=0)
    dgates = dx_sum[:, width : width + experts] + dx_sum[:, width + experts : width + 2 * experts]
    dchosen = (
        named * (dgates - jnp.sum(dgates * gates, axis=1, keepdims=True)) / chosen_sum
    )
    dlogits = (probs * (dchosen - jnp.sum(probs * dchosen, axis=1, keepdims=True))).astype(BF)
    grad_router = dot_first(n2, dlogits)
    dn2 = dx_sum[:, :width] + dot_last(dlogits, router_w)
    upstream = cotangent.astype(F32)
    grad_gain_two = jnp.sum(dn2 * nu_two, axis=0)
    scaled = dn2 * gain_two
    dhidden = upstream + r_two * (
        scaled - nu_two * jnp.mean(scaled * nu_two, axis=-1, keepdims=True)
    )
    da = (live * dhidden).astype(BF)
    gain_size = norm_gains.shape[0]
    grad_router = grad_router.reshape(n, router_rows, 128)
    if small:
        dn1, r_back, gws, goo, gor, gol, grs, gvs, *_ = back(
            n_e,
            n_z,
            cap,
            heads,
            da,
            r_rows,
            r_far,
            grad_router,
            n1,
            raw,
            value,
            mix,
            unpicks,
            grad_gain_two[None],
            *shape,
        )
        gw_sum = gws.astype(F32).transpose(0, 2, 1, 3).reshape(n_e, shard, -1)
        lower_sum, upper_sum = (
            jnp.where(came, lax.dynamic_index_in_dim(inbox, z, keepdims=False).astype(F32), 0.0)
            for came, inbox in ((z > 0, gor), (z < n_z - 1, gol))
        )
        grad_out = goo.astype(F32) + lower_sum + upper_sum
        grad_router = jnp.sum(grs, axis=0)
        grad_gains = lax.dynamic_slice_in_dim(
            jnp.sum(gvs, axis=0).reshape(-1), device * gain_size, gain_size
        )
    else:
        r_back = give_back(n_e, n_z, cap, r_rows, unpicks, 7)
        da_all = plane_gather(n_e, n_z, da)
        dn_part, gw, go, g1_part, gh_part = attend_back(
            n_e,
            heads,
            da_all,
            n1,
            raw,
            value,
            mix,
            turn_table,
            seg,
            w_all,
            wo_all,
            gain_heads,
        )
        gain_all = jnp.concatenate(
            [(g1_part / gain_one)[0], grad_gain_two, gh_part[0], gh_part[1]]
        ).reshape(n, -1)
        grad_rows = -(-(router_rows + gain_rows) // 8) * 8
        gain_all = pad_lanes(gain_all, (grad_rows - router_rows) * 128)
        gm = jnp.concatenate([grad_router, gain_all.reshape(n, -1, 128)], axis=1)
        dn1, gws, gos, gms = finish(
            n_e,
            n_z,
            dn_part,
            gw.reshape(n, shard, -1),
            go.reshape(n_z, -1, width),
            gm,
        )
        gw_sum = jnp.sum(gws.reshape(n_e, n_z, shard, -1).astype(F32), axis=1)
        grad_out = jnp.sum(gos.astype(F32), axis=0)
        gm_sum = jnp.sum(gms, axis=0)
        grad_router = gm_sum[:router_rows]
        grad_gains = gm_sum[router_rows:].reshape(-1)[:gain_size]
    block_out = (hidden + jnp.sum(r_back.astype(F32), axis=0)).astype(BF)
    r_one = lax.rsqrt(jnp.mean(inputs * inputs, axis=-1, keepdims=True) + EPSILON)
    nu_one = inputs * r_one
    scaled = dn1 * gain_one
    grad_tokens = dhidden + r_one * (
        scaled - nu_one * jnp.mean(scaled * nu_one, axis=-1, keepdims=True)
    )
    q_size = heads * HEAD
    grad_query = gw_sum[:, :, :q_size].transpose(1, 0, 2).reshape(shard, -1)
    kv_sum = gw_sum[:, :, q_size:].reshape(kv_heads, -1, shard, 2 * HEAD).sum(axis=1)
    grad_key = kv_sum[:, :, :HEAD].transpose(1, 0, 2).reshape(shard, -1)
    grad_value = kv_sum[:, :, HEAD:].transpose(1, 0, 2).reshape(shard, -1)
    return (
        block_out,
        grad_tokens,
        grad_query,
        grad_key,
        grad_value,
        grad_out,
        grad_router.reshape(shard, experts),
        grad_gains,
        grad_gate[None],
        grad_up[None],
        grad_down[None],
    )


def solution(mesh):
    both = ("expert", "fsdp")
    two, three = P(both, None), P(both, None, None)
    return jax.shard_map(
        partial(local, mesh.shape["expert"], mesh.shape["fsdp"]),
        mesh=mesh,
        in_specs=(two, two, P(), P(), two) + (two,) * 5 + (P(both),) + (three,) * 3,
        out_specs=(two,) * 7 + (P(both),) + (three,) * 3,
        check_vma=False,
    )
```

time: 3360 us -> 834 us (0.25)
  waiting for transfers between devices: 2320 us -> 0 us
  Pallas kernels: 0 us -> 761 us
  blocking collectives: 383 us -> 0 us
  matrix products: 246 us -> 7.06 us
  local copies, waits for them, and re-layouts: 173 us -> 16.6 us
  other arithmetic: 178 us -> 39.4 us
    reduce_scatter x4 -> x0, waiting for transfers between devices: 1540 us -> none  [the longest x1 714 us: local(): lax.psum_scatter(grad_terms[0], ('expert', 'fsdp'), scatter_dimension=0,...]
    pallas_call x0 -> x4, Pallas kernels: none -> 761 us  [the longest x1 283 us: moe(): pl.pallas_call(partial(moe_kernel, n_e, n_z, cap), out_shape=(rows_of(col...]
    all_to_all x4 -> x0, waiting for transfers between devices: 555 us -> none  [the longest x1 199 us: send_grads(): lax.all_to_all(buffer, ('expert', 'fsdp'), split_axis=0, concat_axis=0, t...]
    all_gather x1 -> x0, blocking collectives: 293 us -> none  [local(): lax.all_gather(w_router, ('expert', 'fsdp'), axis=0, tiled=True)]
    dot_general x29 -> x5, matrix products: 243 us -> 7.06 us  [the longest x1 3.08 us: dot_last(): lax.dot_general(a, b, (((1,), (1,)), ((), ())), preferred_element_type=F32)]
    all_gather x4 -> x0, waiting for transfers between devices: 230 us -> none  [the longest x1 106 us: local(): lax.all_gather(w_query, ('expert', 'fsdp'), axis=0, tiled=True)]
    gather x8 -> x0, local copies, waits for them, and re-layouts: 119 us -> none  [the longest x1 51.1 us: local(): grad_back[routes, slot_of].astype(jnp.float32) * live_f[:, :, None]]
    unnamed x2 -> x0, blocking collectives: 90.5 us -> none
  transfers between devices with their start and end apart: 13 -> 0, of which waited for: 9 -> 0; matrix products, arithmetic and copies ran while one was open for 15% -> 0% of each run, Pallas kernels for 0% -> 0%
where the time goes in v1:
time: 834 us; the launch traced here: 825 us
  Pallas kernels  761 us (91%)
  other arithmetic  39.4 us (5%)
  local copies, waits for them, and re-layouts  16.6 us (2%)
    pallas_call x1, Pallas kernels, moe(): pl.pallas_call(partial(moe_kernel, n_e, n_z, cap), out_shape=(rows_of(col...  283 us
    pallas_call x1, Pallas kernels, back(): pl.pallas_call(partial(back_kernel, n_e, n_z, cap, heads), out_shape=(jax...  227 us
    pallas_call x1, Pallas kernels, front(): pl.pallas_call(partial(front_kernel, n_e, n_z, cap, heads), out_shape=tup...  148 us
    pallas_call x1, Pallas kernels, open_layer(): pl.pallas_call(partial(open_kernel, n_e, n_z, cap), out_shape=(like(n_e,...  103 us

profile of v1, /device:TPU:0, one launch (start us, length us, event | category | flops | bytes accessed | tf_op | source)
XLA Modules:
  0.0 825.3 jit_solution(9273846767892918082)
XLA Ops:
  3.9 3.7 multiply_cosine_fusion
  7.6 1.3 pad_maximum_fusion.1.turn_ref
  9.0 1.2 fusion.9.pick_ref
  13.1 103.1 %open_layer.1 = (bf16[8,256,2048]{2,1,0:T(8,128)(2,1)}, s32[4,16,128]{2,1,0:T(8,128)}, bf16[8,4,64,768]{3,2,1,0:T(8,128)(2,1)}, bf16[4,128,2048]{2,1,0:T(8,128)(...) custom-call(bf16[256,2048]{1,0:T(8,128)(2,1)} %x_ref.1, bf16[256,2048]{1,0:T(8,128)(2,1)} %ct_ref.3, ...), custom_call_target="tpu_custom_call" | custom-call | tf_op jit(solution)/shard_map/open_layer/pallas_call | solution.py:559
  118.4 1.5 copy.103.pick_ref
  122.0 147.5 %front.1 = (bf16[8,256,2048]{2,1,0:T(8,128)(2,1)}, f32[8,256,640]{2,1,0:T(8,128)}, bf16[8,256,128]{2,1,0:T(8,128)(2,1)}, bf16[8,256,512]{2,1,0:T(8,128)(2,1)}, f...) custom-call(bf16[8,256,2048]{2,1,0:T(8,128)(2,1)} %get-tuple-element.37.xs_ref, bf16[256,2048]{1,0:T(8,128)(2,1)} %ct_ref.3, ...), custom_call_target="tpu_custom_call" | custom-call | tf_op jit(solution)/shard_map/front/pallas_call | solution.py:1170
  269.6 2.2 multiply_reduce_fusion.2
  271.8 1.3 copy-done.2
  275.0 1.1 pad_maximum_fusion.tok_ref
  276.1 282.8 %moe.1 = (bf16[4,8,80,2176]{3,2,1,0:T(8,128)(2,1)}, bf16[4,8,80,2048]{3,2,1,0:T(8,128)(2,1)}, bf16[4,8,80,2176]{3,2,1,0:T(8,128)(2,1)}, bf16[4,8,80,2176]{3,2,1,...) custom-call(bf16[256,2176]{1,0:T(8,128)(2,1)} %pad_maximum_fusion.to, ...), custom_call_target="tpu_custom_call" | custom-call | tf_op jit(solution)/shard_map/moe/pallas_call | solution.py:2400
  558.8 3.2 convert_reduce_fusion
  562.4 1.1 copy-done.14
  563.8 1.6 fusion.54
  565.4 2.2 reshape.318.gr_ref
  567.6 3.1 multiply_reduce_fusion
  570.7 1.7 multiply_convert_fusion.da_ref
  572.4 227.2 %back.1 = (f32[256,2048]{1,0:T(8,128)}, bf16[4,256,2048]{2,1,0:T(8,128)(2,1)}, bf16[8,3,64,256]{3,2,1,0:T(8,128)(2,1)}, bf16[128,2048]{1,0:T(8,128)(2,1)}, bf16[...) custom-call(bf16[256,2048]{1,0:T(8,128)(2,1)} %multiply_convert_fusi, ...), custom_call_target="tpu_custom_call" | custom-call | tf_op jit(solution)/shard_map/back/pallas_call | solution.py:1863
  799.6 2.6 bitcast_add_fusion
  802.2 3.4 convert_reduce_fusion.1
  806.2 1.1 copy-done.4
  807.6 2.9 fusion.5
  814.9 3.5 bitcast_convert_fusion
  818.4 3.2 bitcast_convert_fusion.1
  821.6 3.2 bitcast_convert_fusion.2
  (127 shorter events, 18.0 us)
Async XLA Ops:
  0.6 9.6 %copy-start = (bf16[64,512]{1,0:T(8,128)(2,1)S(1)}, bf16[64,512]{1,0:T(8,128)(2,1)}, u32[]{:S(2)}) copy-start(bf16[64,512]{1,0:T(8,128)(2,1)} %param.20) | copy-start | bytes 196612
  7.6 2.6 copy-start.20
  7.6 2.7 copy-start.25
  8.9 3.2 copy-start.27
  8.9 3.4 copy-start.28
  117.4 2.5 copy-start.22
  118.4 3.0 copy-start.13
  122.0 147.5 %copy-start.9 = (bf16[256,2048]{1,0:T(8,128)(2,1)S(1)}, bf16[256,2048]{1,0:T(8,128)(2,1)}, u32[]{:S(2)}) copy-start(bf16[256,2048]{1,0:T(8,128)(2,1)} %x_ref.1) | copy-start | bytes 3145732
  273.4 2.7 copy-start.11
  558.8 4.9 copy-start.12
  563.4 4.1 copy-start.3
  567.6 3.1 copy-start.7
  802.2 3.5 copy-start.10
  802.2 3.5 copy-start.15
  802.2 3.5 copy-start.23
  802.2 4.0 copy-start.6
  805.6 1.9 copy-start.8
  807.6 2.9 copy-start.19
  810.9 2.5 copy-start.21
  810.9 3.3 copy-start.24
  811.0 3.9 copy-start.18
  814.9 3.6 copy-start.17
  818.4 3.2 copy-start.16
  821.6 3.2 copy-start.1
  (5 other events, 7.5 us)

commit v2 on v1

--- a/solution.py
+++ b/solution.py
@@ -1019,6 +1019,7 @@
     mine,
     sib,
     far,
+    via,
     zbuf,
     rows,
     x_sem,
@@ -1027,6 +1028,8 @@
     sib_recv,
     send,
     recv,
+    via_send,
+    via_recv,
     z_send,
     z_recv,
     r_send,
@@ -1045,6 +1048,23 @@
     def blocks(k):
         j = partner_chip(chip, nc - 1 - k)
         return j, (2 * j + 1 - core, 2 * j + core)
+
+    half = count // 2
+
+    def via_copy(p):
+        rows = pl.ds(pl.multiple_of(p * half, half), half)
+        there = (2 * partner_chip(chip, p + 1) + core, z)
+        return remote(
+            mine.at[partner_chip(chip, nc - 1), rows, :],
+            via.at[p],
+            via_send.at[p],
+            via_recv.at[p],
+            there,
+        )
+
+    def far_copy(p):
+        j = partner_chip(chip, 2 - p)
+        return remote(mine.at[j], far.at[p], send.at[p], recv.at[p], (2 * j + core, z))
 
     def load(b, slot):
         return pltpu.make_async_copy(xs_ref.at[b], xbuf.at[slot], x_sem.at[slot])
@@ -1109,9 +1129,22 @@
                     mine[j, at, :].astype(F32) + sib[j, at, :].astype(F32)
                 ).astype(BF)
 
-            remote(
-                mine.at[j], far.at[chip], send.at[j], recv.at[chip], (2 * j + core, z)
-            ).start()
+        @pl.when(k == 0)
+        def _():
+            for p in range(2):
+                via_copy(p).start()
+
+        @pl.when((k > 0) & (k < nc - 1))
+        def _():
+            via_copy(k - 1).wait_recv()
+
+            @pl.loop(0, half, step=step)
+            def _(r):
+                at = pl.ds(pl.multiple_of((k - 1) * half + r, step), step)
+                came = via[k - 1, pl.ds(pl.multiple_of(r, step), step), :]
+                mine[j, at, :] = (mine[j, at, :].astype(F32) + came.astype(F32)).astype(BF)
+
+            far_copy(k - 1).start()
 
         @pl.when((k > 0) & (k < n_z))
         def _():
@@ -1135,16 +1168,15 @@
         at = pl.ds(pl.multiple_of(r, step), step)
         total_ref[at, :] = mine[chip, at, :].astype(F32) + sib[chip, at, :].astype(F32)
 
-    for k in range(nc - 1, 0, -1):
-        j = partner_chip(chip, k)
-        remote(
-            mine.at[j], far.at[j], send.at[j], recv.at[j], (2 * j + core, z)
-        ).wait()
+    for p in range(2):
+        far_copy(p).wait()
 
         @pl.loop(0, count, step=step)
-        def _(r, j=j):
+        def _(r, p=p):
             at = pl.ds(pl.multiple_of(r, step), step)
-            total_ref[at, :] += far[j, at, :].astype(F32)
+            total_ref[at, :] += far[p, at, :].astype(F32)
+
+        via_copy(p).wait_send()
 
     for slot, b in enumerate(blocks(nc - 1)[1]):
         for copy in stores(b, slot):
@@ -1162,7 +1194,8 @@
     outs = ((width, BF), ((heads + 1) * HEAD, F32), (HEAD, BF), (heads * HEAD, BF))
     bufs = [pltpu.VMEM((2, count, width), BF)]
     bufs += [pltpu.VMEM((2, count, c), t) for c, t in outs]
-    bufs += [pltpu.VMEM((nc, count, width), BF)] * 4
+    bufs += [pltpu.VMEM((nc, count, width), BF)] * 3
+    bufs += [pltpu.VMEM((2, count, width), BF), pltpu.VMEM((2, count // 2, width), BF)]
     bufs += [
         pltpu.VMEM((n_z, count, width), BF),
         pltpu.VMEM((n_z - 1, n_e * cap, width), BF),
@@ -1182,8 +1215,10 @@
             DMA((4, 2)),
             DMA((nc,)),
             DMA((nc,)),
-            DMA((nc,)),
-            DMA((nc,)),
+            DMA((2,)),
+            DMA((2,)),
+            DMA((2,)),
+            DMA((2,)),
             DMA((n_z + 1,)),
             DMA((n_z,)),
             DMA((n_z, n_e)),
@@ -1538,8 +1573,8 @@
                 add(d, inbox)
             remote(block, inbox.at[d], send.at[d], recv.at[d], (e, z + step)).start()
 
-    def pass_all(one_pass, stage):
-        for d in range(n_z - 1):
+    def pass_all(one_pass, stage, steps=range(n_z - 1)):
+        for d in steps:
             one_pass(n_z - 1 - d, 1, stage)
             one_pass(d, -1, stage)
 
@@ -1584,7 +1619,7 @@
     def sum_rows(src, dst, k):
         sz = source(k)
         unpick = unpick_ref[sz]
-        cuts = pieces(width, 256)
+        cuts = pieces(width)
 
         def fetch(p):
             start, size = cuts[p]
@@ -1643,14 +1678,9 @@
                 da_ref, das.at[pair[1]], ds_send.at[k], ds_recv.at[j], sibling
             ).wait_recv()
 
-        @pl.when(k == nc - 1)
-        def _():
-            sibling_da()
-            out_weights()
-
         for slot, b in enumerate(pair):
             if slot == 1:
-                pl.when(k < nc - 1)(sibling_da)
+                sibling_da()
             load_raw(b, slot).wait()
             part = attend_back_block(
                 heads,
@@ -1719,10 +1749,6 @@
         remote(block, block, ds_send.at[k], ds_recv.at[chip], sibling).wait_send()
 
     give_rows(0)
-    pltpu.make_async_copy(gob.at[z], goo_ref, own.at[3]).start()
-    pass_all(out_pass, 1)
-    take_rows(n_z - 2)
-    send_sum(n_z - 2).start()
 
     dcat = dcats[...].reshape(tokens, -1)
 
@@ -1734,7 +1760,8 @@
             n1s[p, :, at] = rows[:, p * n_z * shard : (p + 1) * n_z * shard]
 
     pass_all(weight_pass, 0)
-
+    out_weights()
+    pltpu.make_async_copy(gob.at[z], goo_ref, own.at[3]).start()
     lanes = 128
     g1 = gsum[...] / g1_ref[...]
     per = width // lanes
@@ -1747,6 +1774,35 @@
         oe = lax.rem(e + i, n_e)
         remote(gvec, gplane.at[e], v_send.at[i], v_recv.at[e], (oe, z)).start()
     gplane[e] = gvec[...]
+    pass_all(weight_pass, 1, range(1))
+    take_rows(n_z - 2)
+    send_sum(n_z - 2).start()
+    pass_all(weight_pass, 1, range(1, n_z - 1))
+    pass_all(weight_pass, 2)
+    for k in range(n_z - 3, 0, -1):
+        take_rows(k)
+        send_sum(k).start()
+    pass_all(out_pass, 1)
+
+    for came, inbox, recv_w, there in (
+        (z > 0, gwr_ref, wr_recv, z - 1),
+        (z < n_z - 1, gwl_ref, wl_recv, z + 1),
+    ):
+
+        @pl.when(came)
+        def _(inbox=inbox, recv_w=recv_w, there=there):
+            block = n1s.at[0:parts, shard_at(z), :]
+            remote(block, inbox.at[z], w_send.at[z], recv_w.at[z], (e, there)).wait_recv()
+            weight_add(z, inbox)
+
+    def weight_block(t):
+        at = pl.ds(pl.multiple_of(t * n_z * shard, n_z * shard), n_z * shard)
+        return n1s.at[0:parts, shard_at(z), at]
+
+    for i in range(1, n_e):
+        oe = lax.rem(e + i, n_e)
+        remote(weight_block(oe), gws_ref.at[e], s_send.at[i], s_recv.at[e], (oe, z)).start()
+    pltpu.make_async_copy(weight_block(e), gws_ref.at[e], own.at[2]).start()
     for k in range(1, nc):
         j = partner_chip(chip, k)
         remote(
@@ -1759,33 +1815,6 @@
             total_ref[at, :] += far[k - 1, at, :].astype(F32)
 
     pass_all(out_pass, 2)
-    for k in range(n_z - 3, 0, -1):
-        take_rows(k)
-        send_sum(k).start()
-    pass_all(weight_pass, 1)
-    take_rows(0)
-    pltpu.make_async_copy(das.at[0], part_ref.at[z], own.at[6]).start()
-    pass_all(weight_pass, 2)
-
-    for came, inbox, recv_w, there in (
-        (z > 0, gwr_ref, wr_recv, z - 1),
-        (z < n_z - 1, gwl_ref, wl_recv, z + 1),
-    ):
-
-        @pl.when(came)
-        def _(inbox=inbox, recv_w=recv_w, there=there):
-            block = n1s.at[0:parts, shard_at(z), :]
-            remote(block, inbox.at[z], w_send.at[z], recv_w.at[z], (e, there)).wait_recv()
-            weight_add(z, inbox)
-
-    def weight_block(t):
-        at = pl.ds(pl.multiple_of(t * n_z * shard, n_z * shard), n_z * shard)
-        return n1s.at[0:parts, shard_at(z), at]
-
-    for i in range(1, n_e):
-        oe = lax.rem(e + i, n_e)
-        remote(weight_block(oe), gws_ref.at[e], s_send.at[i], s_recv.at[e], (oe, z)).start()
-    pltpu.make_async_copy(weight_block(e), gws_ref.at[e], own.at[2]).start()
     for i in range(1, n_e):
         oe = lax.rem(e + i, n_e)
         remote(gvec, gplane.at[oe], v_send.at[i], v_recv.at[oe], (oe, z)).wait()
@@ -1795,6 +1824,8 @@
         remote(gtotal, gvs_ref.at[z], vz_send.at[k], vz_recv.at[z], (e, oz)).start()
     own_gv = pltpu.make_async_copy(gtotal, gvs_ref.at[z], own.at[4])
     own_gv.start()
+    take_rows(0)
+    pltpu.make_async_copy(das.at[0], part_ref.at[z], own.at[6]).start()
 
     @pl.loop(1, n)
     def _(k):
@@ -1895,7 +1926,7 @@
             pltpu.VMEM((nc,) + block, BF),
             pltpu.VMEM((2,) + block, BF),
             pltpu.VMEM((nc - 1,) + block, BF),
-            pltpu.VMEM((2, n_e, cap, 256), BF),
+            pltpu.VMEM((2, n_e, cap, pieces(width)[0][1]), BF),
             pltpu.VMEM((n_z, wo.shape[0] // n_z, width), BF),
             sems(7),
             sems(3),

time: 834 us -> 818 us (0.981)
  Pallas kernels: 761 us -> 745 us
    pallas_call x1, Pallas kernels: 148 us -> 138 us  [front(): pl.pallas_call(partial(front_kernel, n_e, n_z, cap, heads), out_shape=tup...]
where the time goes in v2:
time: 818 us; the launch traced here: 810 us
  Pallas kernels  745 us (91%)
  other arithmetic  39.4 us (5%)
  local copies, waits for them, and re-layouts  16.6 us (2%)
    pallas_call x1, Pallas kernels, moe(): pl.pallas_call(partial(moe_kernel, n_e, n_z, cap), out_shape=(rows_of(col...  284 us
    pallas_call x1, Pallas kernels, back(): pl.pallas_call(partial(back_kernel, n_e, n_z, cap, heads), out_shape=(jax...  220 us
    pallas_call x1, Pallas kernels, front(): pl.pallas_call(partial(front_kernel, n_e, n_z, cap, heads), out_shape=tup...  138 us
    pallas_call x1, Pallas kernels, open_layer(): pl.pallas_call(partial(open_kernel, n_e, n_z, cap), out_shape=(like(n_e,...  103 us

profile of v2, /device:TPU:0, one launch (start us, length us, event | category | flops | bytes accessed | tf_op | source)
XLA Modules:
  0.0 810.3 jit_solution(879457682760347586)
XLA Ops:
  3.9 3.7 multiply_cosine_fusion
  7.6 1.3 pad_maximum_fusion.1.turn_ref
  9.0 1.2 fusion.9.pick_ref
  13.1 103.1 %open_layer.1 = (bf16[8,256,2048]{2,1,0:T(8,128)(2,1)}, s32[4,16,128]{2,1,0:T(8,128)}, bf16[8,4,64,768]{3,2,1,0:T(8,128)(2,1)}, bf16[4,128,2048]{2,1,0:T(8,128)(...) custom-call(bf16[256,2048]{1,0:T(8,128)(2,1)} %x_ref.1, bf16[256,2048]{1,0:T(8,128)(2,1)} %ct_ref.3, ...), custom_call_target="tpu_custom_call" | custom-call | tf_op jit(solution)/shard_map/open_layer/pallas_call | solution.py:559
  118.4 1.5 copy.103.pick_ref
  122.0 138.4 %front.1 = (bf16[8,256,2048]{2,1,0:T(8,128)(2,1)}, f32[8,256,640]{2,1,0:T(8,128)}, bf16[8,256,128]{2,1,0:T(8,128)(2,1)}, bf16[8,256,512]{2,1,0:T(8,128)(2,1)}, f...) custom-call(bf16[8,256,2048]{2,1,0:T(8,128)(2,1)} %get-tuple-element.37.xs_ref, bf16[256,2048]{1,0:T(8,128)(2,1)} %ct_ref.3, ...), custom_call_target="tpu_custom_call" | custom-call | tf_op jit(solution)/shard_map/front/pallas_call | solution.py:1203
  260.5 2.2 multiply_reduce_fusion.2
  262.7 1.3 copy-done.2
  265.9 1.1 pad_maximum_fusion.tok_ref
  267.0 284.1 %moe.1 = (bf16[4,8,80,2176]{3,2,1,0:T(8,128)(2,1)}, bf16[4,8,80,2048]{3,2,1,0:T(8,128)(2,1)}, bf16[4,8,80,2176]{3,2,1,0:T(8,128)(2,1)}, bf16[4,8,80,2176]{3,2,1,...) custom-call(bf16[256,2176]{1,0:T(8,128)(2,1)} %pad_maximum_fusion.to, ...), custom_call_target="tpu_custom_call" | custom-call | tf_op jit(solution)/shard_map/moe/pallas_call | solution.py:2431
  551.1 3.2 convert_reduce_fusion
  554.6 1.1 copy-done.14
  556.0 1.6 fusion.54
  557.6 2.2 reshape.318.gr_ref
  559.8 3.1 multiply_reduce_fusion
  562.9 1.7 multiply_convert_fusion.da_ref
  564.6 219.9 %back.1 = (f32[256,2048]{1,0:T(8,128)}, bf16[4,256,2048]{2,1,0:T(8,128)(2,1)}, bf16[8,3,64,256]{3,2,1,0:T(8,128)(2,1)}, bf16[128,2048]{1,0:T(8,128)(2,1)}, bf16[...) custom-call(bf16[256,2048]{1,0:T(8,128)(2,1)} %multiply_convert_fusi, ...), custom_call_target="tpu_custom_call" | custom-call | tf_op jit(solution)/shard_map/back/pallas_call | solution.py:1894
  784.5 2.6 bitcast_add_fusion
  787.1 3.4 convert_reduce_fusion.1
  791.1 1.1 copy-done.4
  792.5 2.9 fusion.5
  799.8 3.5 bitcast_convert_fusion
  803.4 3.2 bitcast_convert_fusion.1
  806.6 3.2 bitcast_convert_fusion.2
  (127 shorter events, 18.0 us)
Async XLA Ops:
  0.6 9.6 %copy-start = (bf16[64,512]{1,0:T(8,128)(2,1)S(1)}, bf16[64,512]{1,0:T(8,128)(2,1)}, u32[]{:S(2)}) copy-start(bf16[64,512]{1,0:T(8,128)(2,1)} %param.20) | copy-start | bytes 196612
  7.6 2.6 copy-start.20
  7.6 2.7 copy-start.25
  8.9 3.2 copy-start.27
  8.9 3.4 copy-start.28
  117.4 2.5 copy-start.22
  118.4 3.0 copy-start.13
  122.0 138.4 %copy-start.9 = (bf16[256,2048]{1,0:T(8,128)(2,1)S(1)}, bf16[256,2048]{1,0:T(8,128)(2,1)}, u32[]{:S(2)}) copy-start(bf16[256,2048]{1,0:T(8,128)(2,1)} %x_ref.1) | copy-start | bytes 3145732
  264.3 2.7 copy-start.11
  551.0 4.9 copy-start.12
  555.7 4.1 copy-start.3
  559.8 3.1 copy-start.7
  787.1 3.5 copy-start.10
  787.1 3.5 copy-start.15
  787.1 3.5 copy-start.23
  787.1 4.0 copy-start.6
  790.6 1.9 copy-start.8
  792.5 2.9 copy-start.19
  795.9 2.5 copy-start.21
  795.9 3.3 copy-start.24
  795.9 3.9 copy-start.18
  799.8 3.6 copy-start.17
  803.4 3.2 copy-start.16
  806.6 3.2 copy-start.1
  (5 other events, 7.5 us)

commit v3 on v2

--- a/solution.py
+++ b/solution.py
@@ -1528,7 +1528,7 @@
 
     def blocks(k):
         j = partner_chip(chip, k)
-        return j, (2 * j + core, 2 * j + 1 - core)
+        return j, (2 * j + 1 - core, 2 * j + core)
 
     def source(k):
         return jnp.where(k == 0, z, ranked(z, k, n_z))
@@ -1659,28 +1659,17 @@
     sum_rows(rfar_ref, rsum, n_z - 1)
     send_sum(n_z - 1).start()
 
+    pltpu.make_async_copy(da_ref, das.at[e], own.at[0]).wait()
+
     @pl.loop(0, nc)
     def _(k):
         j, pair = blocks(k)
-
-        @pl.when(k == 0)
-        def _():
-            pltpu.make_async_copy(da_ref, das.at[e], own.at[0]).wait()
-
-        @pl.when(k > 0)
-        def _():
-            block = das.at[2 * j + core]
-            remote(da_ref, block, d_send.at[k], d_recv.at[j], far_chip(k)).wait_recv()
-            remote(block, block, ds_send.at[k], ds_recv.at[j], sibling).start()
-
-        def sibling_da():
-            remote(
-                da_ref, das.at[pair[1]], ds_send.at[k], ds_recv.at[j], sibling
-            ).wait_recv()
-
+        remote(da_ref, das.at[pair[0]], ds_send.at[k], ds_recv.at[j], sibling).wait_recv()
+        pl.when(k == nc - 1)(out_weights)
+        to_sibling = remote(
+            away, sib.at[lax.rem(k, 2)], sib_send, sib_recv.at[lax.rem(k, 2)], sibling
+        )
         for slot, b in enumerate(pair):
-            if slot == 1:
-                sibling_da()
             load_raw(b, slot).wait()
             part = attend_back_block(
                 heads,
@@ -1703,18 +1692,24 @@
             def _(slot=slot):
                 load_raw(blocks(k + 1)[1][slot], slot).start()
 
-            if slot == 0:
+            if slot == 1:
                 mine[j] = part
-            else:
-                away[...] = part
-        to_sibling = remote(
-            away, sib.at[lax.rem(k, 2)], sib_send, sib_recv.at[lax.rem(k, 2)], sibling
-        )
-        to_sibling.start()
-
-        @pl.when(k == 0)
-        def _():
-            give_da(nc - 1).start()
+                continue
+            away[...] = part
+            to_sibling.start()
+
+            @pl.when(k == 0)
+            def _():
+                give_da(nc - 1).start()
+
+            @pl.when(k < nc - 1)
+            def _():
+                nj = blocks(k + 1)[0]
+                block = das.at[2 * nj + core]
+                remote(
+                    da_ref, block, d_send.at[k + 1], d_recv.at[nj], far_chip(k + 1)
+                ).wait_recv()
+                remote(block, block, ds_send.at[k + 1], ds_recv.at[nj], sibling).start()
 
         @pl.when((k > 0) & (k < n_z - 1))
         def _():
@@ -1760,7 +1755,6 @@
             n1s[p, :, at] = rows[:, p * n_z * shard : (p + 1) * n_z * shard]
 
     pass_all(weight_pass, 0)
-    out_weights()
     pltpu.make_async_copy(gob.at[z], goo_ref, own.at[3]).start()
     lanes = 128
     g1 = gsum[...] / g1_ref[...]
@@ -1774,15 +1768,16 @@
         oe = lax.rem(e + i, n_e)
         remote(gvec, gplane.at[e], v_send.at[i], v_recv.at[e], (oe, z)).start()
     gplane[e] = gvec[...]
+    pass_all(out_pass, 1)
+    take_rows(n_z - 2)
     pass_all(weight_pass, 1, range(1))
-    take_rows(n_z - 2)
     send_sum(n_z - 2).start()
+    pass_all(out_pass, 2)
     pass_all(weight_pass, 1, range(1, n_z - 1))
-    pass_all(weight_pass, 2)
     for k in range(n_z - 3, 0, -1):
         take_rows(k)
         send_sum(k).start()
-    pass_all(out_pass, 1)
+    pass_all(weight_pass, 2)
 
     for came, inbox, recv_w, there in (
         (z > 0, gwr_ref, wr_recv, z - 1),
@@ -1814,7 +1809,6 @@
             at = pl.ds(pl.multiple_of(r, step), step)
             total_ref[at, :] += far[k - 1, at, :].astype(F32)
 
-    pass_all(out_pass, 2)
     for i in range(1, n_e):
         oe = lax.rem(e + i, n_e)
         remote(gvec, gplane.at[oe], v_send.at[i], v_recv.at[oe], (oe, z)).wait()
@@ -2271,11 +2265,11 @@
             r_ref.at[far_z, oe], rret_ref.at[e], e_send.at[i], e_recv.at[e], (oe, z)
         )
 
+    give(0)
     for i in range(1, n_e):
         give_result(i).start()
     own_result = pltpu.make_async_copy(r_ref.at[far_z, e], rret_ref.at[e], in_sem.at[0])
     own_result.start()
-    give(0)
     size = 256
     count = width // size
 

time: 818 us -> 806 us (0.985)
  Pallas kernels: 745 us -> 732 us
where the time goes in v3:
time: 806 us; the launch traced here: 797 us
  Pallas kernels  732 us (91%)
  other arithmetic  39.4 us (5%)
  local copies, waits for them, and re-layouts  16.6 us (2%)
    pallas_call x1, Pallas kernels, moe(): pl.pallas_call(partial(moe_kernel, n_e, n_z, cap), out_shape=(rows_of(col...  279 us
    pallas_call x1, Pallas kernels, back(): pl.pallas_call(partial(back_kernel, n_e, n_z, cap, heads), out_shape=(jax...  212 us
    pallas_call x1, Pallas kernels, front(): pl.pallas_call(partial(front_kernel, n_e, n_z, cap, heads), out_shape=tup...  138 us
    pallas_call x1, Pallas kernels, open_layer(): pl.pallas_call(partial(open_kernel, n_e, n_z, cap), out_shape=(like(n_e,...  103 us

profile of v3, /device:TPU:0, one launch (start us, length us, event | category | flops | bytes accessed | tf_op | source)
XLA Modules:
  0.0 797.0 jit_solution(17882602294893156633)
XLA Ops:
  3.9 3.7 multiply_cosine_fusion
  7.6 1.3 pad_maximum_fusion.1.turn_ref
  9.0 1.2 fusion.9.pick_ref
  13.1 103.1 %open_layer.1 = (bf16[8,256,2048]{2,1,0:T(8,128)(2,1)}, s32[4,16,128]{2,1,0:T(8,128)}, bf16[8,4,64,768]{3,2,1,0:T(8,128)(2,1)}, bf16[4,128,2048]{2,1,0:T(8,128)(...) custom-call(bf16[256,2048]{1,0:T(8,128)(2,1)} %x_ref.1, bf16[256,2048]{1,0:T(8,128)(2,1)} %ct_ref.3, ...), custom_call_target="tpu_custom_call" | custom-call | tf_op jit(solution)/shard_map/open_layer/pallas_call | solution.py:559
  118.4 1.5 copy.103.pick_ref
  122.0 138.4 %front.1 = (bf16[8,256,2048]{2,1,0:T(8,128)(2,1)}, f32[8,256,640]{2,1,0:T(8,128)}, bf16[8,256,128]{2,1,0:T(8,128)(2,1)}, bf16[8,256,512]{2,1,0:T(8,128)(2,1)}, f...) custom-call(bf16[8,256,2048]{2,1,0:T(8,128)(2,1)} %get-tuple-element.37.xs_ref, bf16[256,2048]{1,0:T(8,128)(2,1)} %ct_ref.3, ...), custom_call_target="tpu_custom_call" | custom-call | tf_op jit(solution)/shard_map/front/pallas_call | solution.py:1203
  260.5 2.2 multiply_reduce_fusion.2
  262.7 1.3 copy-done.2
  265.9 1.1 pad_maximum_fusion.tok_ref
  267.0 278.8 %moe.1 = (bf16[4,8,80,2176]{3,2,1,0:T(8,128)(2,1)}, bf16[4,8,80,2048]{3,2,1,0:T(8,128)(2,1)}, bf16[4,8,80,2176]{3,2,1,0:T(8,128)(2,1)}, bf16[4,8,80,2176]{3,2,1,...) custom-call(bf16[256,2176]{1,0:T(8,128)(2,1)} %pad_maximum_fusion.to, ...), custom_call_target="tpu_custom_call" | custom-call | tf_op jit(solution)/shard_map/moe/pallas_call | solution.py:2425
  545.8 3.2 convert_reduce_fusion
  549.4 1.1 copy-done.14
  550.8 1.6 fusion.54
  552.4 2.2 reshape.318.gr_ref
  554.6 3.1 multiply_reduce_fusion
  557.7 1.7 multiply_convert_fusion.da_ref
  559.4 211.9 %back.1 = (f32[256,2048]{1,0:T(8,128)}, bf16[4,256,2048]{2,1,0:T(8,128)(2,1)}, bf16[8,3,64,256]{3,2,1,0:T(8,128)(2,1)}, bf16[128,2048]{1,0:T(8,128)(2,1)}, bf16[...) custom-call(bf16[256,2048]{1,0:T(8,128)(2,1)} %multiply_convert_fusi, ...), custom_call_target="tpu_custom_call" | custom-call | tf_op jit(solution)/shard_map/back/pallas_call | solution.py:1888
  771.3 2.6 bitcast_add_fusion
  773.9 3.4 convert_reduce_fusion.1
  777.9 1.1 copy-done.4
  779.3 2.9 fusion.5
  786.6 3.5 bitcast_convert_fusion
  790.2 3.2 bitcast_convert_fusion.1
  793.4 3.2 bitcast_convert_fusion.2
  (127 shorter events, 18.0 us)
Async XLA Ops:
  0.6 9.6 %copy-start = (bf16[64,512]{1,0:T(8,128)(2,1)S(1)}, bf16[64,512]{1,0:T(8,128)(2,1)}, u32[]{:S(2)}) copy-start(bf16[64,512]{1,0:T(8,128)(2,1)} %param.20) | copy-start | bytes 196612
  7.6 2.6 copy-start.20
  7.6 2.7 copy-start.25
  8.9 3.2 copy-start.27
  8.9 3.4 copy-start.28
  117.4 2.5 copy-start.22
  118.4 3.0 copy-start.13
  122.0 138.4 %copy-start.9 = (bf16[256,2048]{1,0:T(8,128)(2,1)S(1)}, bf16[256,2048]{1,0:T(8,128)(2,1)}, u32[]{:S(2)}) copy-start(bf16[256,2048]{1,0:T(8,128)(2,1)} %x_ref.1) | copy-start | bytes 3145732
  264.3 2.7 copy-start.11
  545.8 4.9 copy-start.12
  550.4 4.1 copy-start.3
  554.6 3.1 copy-start.7
  773.9 3.5 copy-start.10
  773.9 3.5 copy-start.15
  773.9 3.5 copy-start.23
  773.9 4.0 copy-start.6
  777.3 1.9 copy-start.8
  779.3 2.9 copy-start.19
  782.7 2.5 copy-start.21
  782.7 3.3 copy-start.24
  782.7 3.9 copy-start.18
  786.6 3.6 copy-start.17
  790.2 3.2 copy-start.16
  793.3 3.2 copy-start.1
  (5 other events, 7.5 us)

commit v4 on v3

--- a/solution.py
+++ b/solution.py
@@ -1456,6 +1456,8 @@
     raw_sem,
     d_send,
     d_recv,
+    via_send,
+    via_recv,
     ds_send,
     ds_recv,
     a_send,
@@ -1505,6 +1507,11 @@
             da_ref, das.at[e], d_send.at[k], d_recv.at[chip], far_chip(k)
         )
 
+    def via_da(b, p):
+        half = count // 2
+        block = das.at[b, pl.ds(pl.multiple_of(p * half, half), half), :]
+        return remote(block, block, via_send.at[p], via_recv.at[p], far_chip(2 - p))
+
     remote(da_ref, das.at[e], ds_send.at[0], ds_recv.at[chip], sibling).start()
     for k in range(1, nc - 1):
         give_da(k).start()
@@ -1698,18 +1705,26 @@
             away[...] = part
             to_sibling.start()
 
-            @pl.when(k == 0)
+            nb = 2 * blocks(k + 1)[0] + core
+
+            def to_core():
+                block = das.at[nb]
+                nj = nb // 2
+                remote(block, block, ds_send.at[k + 1], ds_recv.at[nj], sibling).start()
+
+            @pl.when(k < nc - 2)
             def _():
-                give_da(nc - 1).start()
-
-            @pl.when(k < nc - 1)
+                remote(
+                    da_ref, das.at[nb], d_send.at[k + 1], d_recv.at[nb // 2], far_chip(k + 1)
+                ).wait_recv()
+                via_da(nb, k).start()
+                to_core()
+
+            @pl.when(k == nc - 2)
             def _():
-                nj = blocks(k + 1)[0]
-                block = das.at[2 * nj + core]
-                remote(
-                    da_ref, block, d_send.at[k + 1], d_recv.at[nj], far_chip(k + 1)
-                ).wait_recv()
-                remote(block, block, ds_send.at[k + 1], ds_recv.at[nj], sibling).start()
+                for p in range(2):
+                    via_da(nb, p).wait_recv()
+                to_core()
 
         @pl.when((k > 0) & (k < n_z - 1))
         def _():
@@ -1738,8 +1753,10 @@
                 total_ref[at, :] = mine[j, at, :].astype(F32) + sib[0, at, :].astype(F32)
 
     remote(da_ref, das.at[e], ds_send.at[0], ds_recv.at[chip], sibling).wait_send()
+    for p in range(2):
+        give_da(p + 1).wait_send()
+        via_da(e, p).wait_send()
     for k in range(1, nc):
-        give_da(k).wait_send()
         block = das.at[2 * partner_chip(chip, k) + core]
         remote(block, block, ds_send.at[k], ds_recv.at[chip], sibling).wait_send()
 
@@ -1927,6 +1944,8 @@
             sems(2),
             sems(nc),
             sems(nc),
+            sems(2),
+            sems(2),
             sems(nc),
             sems(nc),
             sems(n),

time: 806 us -> 804 us (level)
  no operation moved by 1% of the time
where the time goes in v4:
time: 804 us; the launch traced here: 795 us
  Pallas kernels  731 us (91%)
  other arithmetic  39.4 us (5%)
  local copies, waits for them, and re-layouts  16.6 us (2%)
    pallas_call x1, Pallas kernels, moe(): pl.pallas_call(partial(moe_kernel, n_e, n_z, cap), out_shape=(rows_of(col...  279 us
    pallas_call x1, Pallas kernels, back(): pl.pallas_call(partial(back_kernel, n_e, n_z, cap, heads), out_shape=(jax...  210 us
    pallas_call x1, Pallas kernels, front(): pl.pallas_call(partial(front_kernel, n_e, n_z, cap, heads), out_shape=tup...  138 us
    pallas_call x1, Pallas kernels, open_layer(): pl.pallas_call(partial(open_kernel, n_e, n_z, cap), out_shape=(like(n_e,...  103 us

profile of v4, /device:TPU:0, one launch (start us, length us, event | category | flops | bytes accessed | tf_op | source)
XLA Modules:
  0.0 795.5 jit_solution(299701293663932658)
XLA Ops:
  3.9 3.7 multiply_cosine_fusion
  7.6 1.3 pad_maximum_fusion.1.turn_ref
  9.0 1.2 fusion.9.pick_ref
  13.1 103.1 %open_layer.1 = (bf16[8,256,2048]{2,1,0:T(8,128)(2,1)}, s32[4,16,128]{2,1,0:T(8,128)}, bf16[8,4,64,768]{3,2,1,0:T(8,128)(2,1)}, bf16[4,128,2048]{2,1,0:T(8,128)(...) custom-call(bf16[256,2048]{1,0:T(8,128)(2,1)} %x_ref.1, bf16[256,2048]{1,0:T(8,128)(2,1)} %ct_ref.3, ...), custom_call_target="tpu_custom_call" | custom-call | tf_op jit(solution)/shard_map/open_layer/pallas_call | solution.py:559
  118.4 1.5 copy.103.pick_ref
  122.0 138.4 %front.1 = (bf16[8,256,2048]{2,1,0:T(8,128)(2,1)}, f32[8,256,640]{2,1,0:T(8,128)}, bf16[8,256,128]{2,1,0:T(8,128)(2,1)}, bf16[8,256,512]{2,1,0:T(8,128)(2,1)}, f...) custom-call(bf16[8,256,2048]{2,1,0:T(8,128)(2,1)} %get-tuple-element.37.xs_ref, bf16[256,2048]{1,0:T(8,128)(2,1)} %ct_ref.3, ...), custom_call_target="tpu_custom_call" | custom-call | tf_op jit(solution)/shard_map/front/pallas_call | solution.py:1203
  260.5 2.2 multiply_reduce_fusion.2
  262.7 1.3 copy-done.2
  265.9 1.1 pad_maximum_fusion.tok_ref
  267.0 278.8 %moe.1 = (bf16[4,8,80,2176]{3,2,1,0:T(8,128)(2,1)}, bf16[4,8,80,2048]{3,2,1,0:T(8,128)(2,1)}, bf16[4,8,80,2176]{3,2,1,0:T(8,128)(2,1)}, bf16[4,8,80,2176]{3,2,1,...) custom-call(bf16[256,2176]{1,0:T(8,128)(2,1)} %pad_maximum_fusion.to, ...), custom_call_target="tpu_custom_call" | custom-call | tf_op jit(solution)/shard_map/moe/pallas_call | solution.py:2444
  545.8 3.2 convert_reduce_fusion
  549.4 1.1 copy-done.14
  550.8 1.6 fusion.54
  552.4 2.2 reshape.318.gr_ref
  554.6 3.1 multiply_reduce_fusion
  557.7 1.7 multiply_convert_fusion.da_ref
  559.4 210.4 %back.1 = (f32[256,2048]{1,0:T(8,128)}, bf16[4,256,2048]{2,1,0:T(8,128)(2,1)}, bf16[8,3,64,256]{3,2,1,0:T(8,128)(2,1)}, bf16[128,2048]{1,0:T(8,128)(2,1)}, bf16[...) custom-call(bf16[256,2048]{1,0:T(8,128)(2,1)} %multiply_convert_fusi, ...), custom_call_target="tpu_custom_call" | custom-call | tf_op jit(solution)/shard_map/back/pallas_call | solution.py:1905
  769.8 2.6 bitcast_add_fusion
  772.4 3.4 convert_reduce_fusion.1
  776.4 1.1 copy-done.4
  777.8 2.9 fusion.5
  785.1 3.5 bitcast_convert_fusion
  788.6 3.2 bitcast_convert_fusion.1
  791.8 3.2 bitcast_convert_fusion.2
  (127 shorter events, 18.0 us)
Async XLA Ops:
  0.6 9.6 %copy-start = (bf16[64,512]{1,0:T(8,128)(2,1)S(1)}, bf16[64,512]{1,0:T(8,128)(2,1)}, u32[]{:S(2)}) copy-start(bf16[64,512]{1,0:T(8,128)(2,1)} %param.20) | copy-start | bytes 196612
  7.6 2.6 copy-start.20
  7.6 2.7 copy-start.25
  8.9 3.2 copy-start.27
  8.9 3.4 copy-start.28
  117.4 2.5 copy-start.22
  118.4 3.0 copy-start.13
  122.0 138.4 %copy-start.9 = (bf16[256,2048]{1,0:T(8,128)(2,1)S(1)}, bf16[256,2048]{1,0:T(8,128)(2,1)}, u32[]{:S(2)}) copy-start(bf16[256,2048]{1,0:T(8,128)(2,1)} %x_ref.1) | copy-start | bytes 3145732
  264.3 2.7 copy-start.11
  545.8 4.9 copy-start.12
  550.4 4.1 copy-start.3
  554.6 3.1 copy-start.7
  772.4 3.5 copy-start.10
  772.4 3.5 copy-start.15
  772.4 3.5 copy-start.23
  772.4 4.0 copy-start.6
  775.8 1.9 copy-start.8
  777.8 2.9 copy-start.19
  781.1 2.5 copy-start.21
  781.1 3.3 copy-start.24
  781.2 3.9 copy-start.18
  785.1 3.6 copy-start.17
  788.6 3.2 copy-start.16
  791.8 3.2 copy-start.1
  (5 other events, 7.5 us)
